TPU v7x, 256 devices: a whole 4x4x8 slice. The times are simulated.
256 devices in a mesh: gx: 8 (over z), gy: 32 (over y, x, core).
Axes of the slice: x: 4, y: 4, z: 8, core: 2. Of those that a mesh axis runs over, the one named last changes fastest.
Arguments:
- bin_population: int32 [256, 1024], P('gy', 'gx'), may hold values from 1 to 16
- local_coordinates: float32 [3, 16, 256, 1024], P(None, None, 'gy', 'gx'), may hold values from 0 to 1
- field_tilt: float32 [2, 16, 256, 1024], P(None, None, 'gy', 'gx'), may hold values from -3.140625 to 3.140625
- body_weights: float32 [16, 256, 1024], P(None, 'gy', 'gx'), may hold values from 0.5 to 2
- thermal_conductance: float32 [16, 256, 1024], P(None, 'gy', 'gx'), may hold values from 1 to 6
- heat_storage: float32 [16, 256, 1024], P(None, 'gy', 'gx'), may hold values from 0.6 to 1.2
- thermal_level: float32 [16, 256, 1024], P(None, 'gy', 'gx'), may hold values from 0.5 to 4
- motion_vectors: float32 [3, 16, 256, 1024], P(None, None, 'gy', 'gx'), may hold values from -0.2 to 0.2
Outputs:
- heated: float32 [16, 256, 1024], P(None, 'gy', 'gx')
- moved: float32 [3, 16, 256, 1024], P(None, None, 'gy', 'gx')
Inputs may be any that keep to these rules, and one draw needn't show every extreme that they name: Slots 0 to bin_population - 1 of a cell hold particles, the others are empty.
All inputs are finite; a program needn't handle non-finite values.
Results may differ from a plain program's by a relative error of at most 0.0001.
Values sent between devices are 32-bit elements; how exact they have to be, the bound alone decides.
A program may use at most 64 MiB of HBM per device.

v0:
```python
import functools

import jax
import jax.numpy as jnp
from jax import lax
from jax.experimental import pallas as pl
from jax.experimental.pallas import tpu as pltpu
from jax.sharding import PartitionSpec as P

SECTIONS = 4
ISO_PART = 0.1
HEAT_RATIO = 5.0 / 3.0
COURANT = 0.3
ROOT_HALF = 0.5**0.5
MESH = pl.DeviceIdType.MESH

SLOTS = 16
ROWS = 8
COLS = 128
FLAT = SLOTS * ROWS

X, Y, Z, BX, BY, BZ, KA, F, M, VX, VY, VZ = range(12)
QUANTITIES = 12

DIRS = ((0, 1), (1, -1), (1, 0), (1, 1))

CO, KE, WX, WY, WZ = range(5)
SELF_AT = len(DIRS) * SLOTS * SLOTS
ROW_AT = SELF_AT + SLOTS * 8
COL_AT = ROW_AT + 6 * SLOTS * 2
PAIRS = COL_AT + 12

EX_Y1, EX_G, EX_Y2, EX_Y3, EX_P = range(5)
EXCHANGES = ((EX_Y1, 2), (EX_Y2, 1), (EX_Y3, 1), (EX_P, 1))

EMPTY_Z = 10.0
OUTSIDE_Z = 20.0
EDGE_Z = 40.0

SIN = (0.9999999957157406, -0.1666665796974384, 0.008333050613415454, -0.0001980904606136566, 2.605165590448684e-06)
COS = (
    0.9999999997798981,
    -0.4999999935694129,
    0.04166663620835954,
    -0.001388836083517328,
    2.476013513307355e-05,
    -2.605106944029617e-07,
)


def rkl_table(section_total):
    weight = 4.0 / (section_total * section_total + section_total - 2)
    series = [1.0 / 3.0, 1.0 / 3.0, 1.0 / 3.0]
    for j in range(3, section_total + 1):
        series.append((j * j + j - 2) / (2.0 * j * (j + 1)))
    rows = []
    for j in range(2, section_total + 1):
        m = (2 * j - 1) / j * series[j] / series[j - 1]
        n = -(j - 1) / j * series[j] / series[j - 2]
        rows.append((m, n, m * weight, -(1.0 - series[j - 1]) * m * weight))
    return series[1] * weight, rows


def horner(coefs, t):
    total = jnp.full_like(t, coefs[-1])
    for c in coefs[-2::-1]:
        total = total * t + c
    return total


def sin_cos(angle):
    half = 0.5 * angle
    t = half * half
    s = half * horner(SIN, t)
    c = horner(COS, t)
    return 2.0 * s * c, 1.0 - 2.0 * s * s


def pair_terms(i, j):
    dx, dy, dz = i[X] - j[X], i[Y] - j[Y], i[Z] - j[Z]
    s = jnp.maximum(1.0 - (dx * dx + dy * dy + dz * dz), 0.0)
    s2 = s * s
    ke = s2 * s
    own = i[BX] * dx + i[BY] * dy + i[BZ] * dz
    far = j[BX] * dx + j[BY] * dy + j[BZ] * dz
    co = ke * (ISO_PART + (own * own + far * far)) * (i[KA] + j[KA])
    w = s2 * (i[M] * j[M])
    return co, ke, w * dx, w * dy, w * dz


def kernel(
    sizes,
    pop,
    loc,
    tilt,
    mass,
    kappa,
    cap,
    temp,
    mot,
    heated,
    moved,
    own,
    far,
    ycur,
    yprev,
    lap0,
    gfac,
    press,
    sfar,
    acc,
    accj,
    kacc,
    kaccj,
    store,
    rowsend0,
    rowrecv0,
    colsend0,
    colrecv0,
    cbsend,
    cbrecv,
    rowfar,
    colfar,
    colown,
    rsend,
    rrecv,
    vsend,
    vrecv,
    drecv,
    hs,
    cf,
    oc,
    msrc,
    mrecv,
    send_sem,
    recv_sem,
    msend_sem,
    mrecv_sem,
):
    n_gx, n_lo, n_hi = sizes
    n_gy = n_lo * n_hi
    gx = lax.axis_index("gx")
    gy = lax.axis_index("gy")
    left, right = lax.rem(gx + n_gx - 1, n_gx), lax.rem(gx + 1, n_gx)
    up, down = lax.rem(gy + n_gy - 1, n_gy), lax.rem(gy + 1, n_gy)
    lo, hi = lax.rem(gy, n_lo), lax.div(gy, n_lo)

    around = ((gx, up), (gx, down), (left, gy), (right, gy), (left, up), (right, up), (left, down), (right, down))
    stages = (
        [(lax.rem(gx + k, n_gx), gy) for k in range(1, n_gx)],
        [(gx, hi * n_lo + lax.rem(lo + k, n_lo)) for k in range(1, n_lo)],
        [(gx, lax.rem(hi + k, n_hi) * n_lo + lo) for k in range(1, n_hi)],
    )

    barrier = pltpu.get_barrier_semaphore()
    greeted = list(around) + [d for stage in stages for d in stage]
    for device in greeted:
        pl.semaphore_signal(barrier, inc=1, device_id=device, device_id_type=MESH)

    lane = lax.broadcasted_iota(jnp.int32, (ROWS, COLS), 1)
    row = lax.broadcasted_iota(jnp.int32, (ROWS, COLS), 0)
    lane16 = lax.broadcasted_iota(jnp.int32, (SLOTS, COLS), 1)
    zero = jnp.zeros((ROWS, COLS), jnp.float32)

    def at(p):
        start = p * ROWS
        return pl.ds(start if isinstance(p, int) else pl.multiple_of(start, ROWS), ROWS)

    def edge_row(side):
        return pl.ds(0 if side == 0 else ROWS - 1, SLOTS, stride=ROWS)

    def shifted(v):
        low = pltpu.roll(v, ROWS - 1, 0)
        return (pltpu.roll(v, COLS - 1, 1), pltpu.roll(low, 1, 1), low, pltpu.roll(low, COLS - 1, 1))

    def unshifted(a, b, c, d):
        return pltpu.roll(a, 1, 1) + pltpu.roll(pltpu.roll(b, COLS - 1, 1) + c + pltpu.roll(d, 1, 1), 1, 0)

    def gather(v, index):
        return jnp.take_along_axis(v, index, axis=1)

    def packed_columns(tile_of):
        v = tile_of(0)
        for p in range(1, SLOTS):
            mask = (lane == 8 * p) | (lane == 8 * p - 1)
            v = jnp.where(mask, pltpu.roll(tile_of(p), 8 * p, 1), v)
        return v

    group = lane & ~7
    within = (lane & 7) * 8
    own_index = (group, (group + (COLS - 1)) & (COLS - 1))
    far_index = (
        ((within + (COLS - 1)) & (COLS - 1), (within + 63) & (COLS - 1)),
        (within, within + 64),
    )

    def prepare(p, fastest):
        live = p < pop[...]
        sin_p, cos_p = sin_cos(tilt[0, p])
        sin_a, cos_a = sin_cos(tilt[1, p])
        t = temp[p]
        v = [mot[c, p] for c in range(3)]
        values = [
            loc[0, p],
            loc[1, p],
            jnp.where(live, loc[2, p], EMPTY_Z),
            ROOT_HALF * (sin_p * cos_a),
            ROOT_HALF * (sin_p * sin_a),
            ROOT_HALF * cos_p,
            0.5 * kappa[p],
            t,
            mass[p],
        ] + v
        for k in range(QUANTITIES):
            own[k, at(p), :] = values[k]
        speed = jnp.sqrt(HEAT_RATIO * (HEAT_RATIO - 1.0) * t) + jnp.sqrt(v[0] * v[0] + v[1] * v[1] + v[2] * v[2])
        return jnp.maximum(fastest, jnp.where(live, speed, 0.0))

    msrc[0] = lax.fori_loop(0, SLOTS, prepare, zero)

    for side in range(2):
        cb = jnp.zeros((SLOTS, COLS), jnp.float32)
        for k in range(QUANTITIES):
            packed = own[k, edge_row(side), :]
            rowsend0[side, k] = packed
            cb = jnp.where((lane16 == 2 * k) | (lane16 == 2 * k + 1), pltpu.roll(packed, 2 * k + 1, 1), cb)
        cbsend[side] = cb

    def pack_k(k, carry):
        colsend0[k] = packed_columns(lambda p: own[k, at(p), :])
        return carry

    lax.fori_loop(0, QUANTITIES, pack_k, 0)

    def remote(src, dst, s, r, device):
        return pltpu.make_async_remote_copy(
            src_ref=src, dst_ref=dst, send_sem=s, recv_sem=r, device_id=device, device_id_type=MESH
        )

    stage_at = (0, n_gx - 1, n_gx + n_lo - 2)

    def stage_copies(stage):
        return [
            remote(
                msrc.at[stage],
                mrecv.at[stage_at[stage] + k],
                msend_sem.at[stage_at[stage] + k],
                mrecv_sem.at[stage_at[stage] + k],
                device,
            )
            for k, device in enumerate(stages[stage])
        ]

    def stage_start(stage):
        for copy in stage_copies(stage):
            copy.start()

    def stage_finish(stage):
        best = msrc[stage]
        for k, copy in enumerate(stage_copies(stage)):
            copy.wait_recv()
            best = jnp.maximum(best, mrecv[stage_at[stage] + k])
        msrc[stage + 1] = best

    def opening_copies():
        plan = (
            (rowsend0.at[0], rowrecv0.at[1]),
            (rowsend0.at[1], rowrecv0.at[0]),
            (colsend0, colrecv0.at[1]),
            (colsend0, colrecv0.at[0]),
            (cbsend.at[0], cbrecv.at[3]),
            (cbsend.at[0], cbrecv.at[2]),
            (cbsend.at[1], cbrecv.at[1]),
            (cbsend.at[1], cbrecv.at[0]),
        )
        return [
            remote(src, dst, send_sem.at[0, c], recv_sem.at[0, c], around[c]) for c, (src, dst) in enumerate(plan)
        ]

    def section_copies(e):
        first, count = EXCHANGES[e - 1]
        part = pl.ds(first, count)
        plan = (
            (rsend.at[0, part], rrecv.at[1, part]),
            (rsend.at[1, part], rrecv.at[0, part]),
            (vsend.at[part], vrecv.at[1, part]),
            (vsend.at[part], vrecv.at[0, part]),
            (rsend.at[0, part], drecv.at[3, part]),
            (rsend.at[0, part], drecv.at[2, part]),
            (rsend.at[1, part], drecv.at[1, part]),
            (rsend.at[1, part], drecv.at[0, part]),
        )
        return [
            remote(src, dst, send_sem.at[e, c], recv_sem.at[e, c], around[c]) for c, (src, dst) in enumerate(plan)
        ]

    pl.semaphore_wait(barrier, len(greeted))
    for copy in opening_copies():
        copy.start()
    stage_start(0)

    def make_far(p, carry):
        for k in range(QUANTITIES):
            for d, v in enumerate(shifted(own[k, at(p), :])):
                if k == X and DIRS[d][1]:
                    v = v + float(DIRS[d][1])
                if k == Y and DIRS[d][0]:
                    v = v + float(DIRS[d][0])
                if k == Z:
                    out = None
                    for step, index, ends in ((DIRS[d][0], row, ROWS - 1), (DIRS[d][1], lane, COLS - 1)):
                        if step:
                            hit = index == (ends if step > 0 else 0)
                            out = hit if out is None else out | hit
                    v = jnp.where(out, OUTSIDE_Z, v)
                far[d, k, p] = v
        for c in range(2):
            acc[c, at(p), :] = zero
            for d in range(4):
                accj[d, c, p] = zero
        for c in range(3):
            kacc[c, at(p), :] = zero
            for d in range(4):
                kaccj[d, c, p] = zero
        return carry

    lax.fori_loop(0, SLOTS, make_far, 0)

    PASS1 = range(9)

    def put(index, terms):
        for c in range(5):
            store[c, index] = terms[c]

    def first_dirs(n, carry):
        d = lax.div(n, 8)
        p0 = lax.rem(n, 8) * 2
        mine = [[own[k, at(p0 + a), :] for k in PASS1] for a in range(2)]
        ti = [zero, zero]
        ri = [zero, zero]
        for q in range(SLOTS):
            other = [far[d, k, q] for k in PASS1]
            tj, rj = None, None
            for a in range(2):
                terms = pair_terms(mine[a], other)
                put(d * 256 + (p0 + a) * 16 + q, terms)
                t = terms[CO] * (other[F] - mine[a][F])
                ti[a] = ti[a] + t
                ri[a] = ri[a] + terms[KE] * other[M]
                r = terms[KE] * mine[a][M]
                tj = t if tj is None else tj + t
                rj = r if rj is None else rj + r
            accj[d, 0, q] = accj[d, 0, q] - tj
            accj[d, 1, q] = accj[d, 1, q] + rj
        for a in range(2):
            acc[0, at(p0 + a), :] += ti[a]
            acc[1, at(p0 + a), :] += ri[a]
        return carry

    def first_self_some(steps):
        def first_self(p, carry):
            mine = [own[k, at(p), :] for k in PASS1]
            ti, ri = zero, zero
            for step in steps:
                q = lax.rem(p + step, SLOTS)
                other = [own[k, at(q), :] for k in PASS1]
                terms = pair_terms(mine, other)
                put(SELF_AT + p * 8 + (step - 1), terms)
                t = terms[CO] * (other[F] - mine[F])
                ti = ti + t
                ri = ri + terms[KE] * other[M]
                acc[0, at(q), :] += -t
                acc[1, at(q), :] += terms[KE] * mine[M]
            acc[0, at(p), :] += ti
            acc[1, at(p), :] += ri
            return carry

        return first_self

    stage_finish(0)
    stage_start(1)
    lax.fori_loop(0, 16, first_dirs, 0)
    stage_finish(1)
    stage_start(2)
    lax.fori_loop(16, 32, first_dirs, 0)
    lax.fori_loop(0, SLOTS, first_self_some(range(1, 8)), 0)
    lax.fori_loop(0, SLOTS // 2, first_self_some((8,)), 0)
    stage_finish(2)

    for copy in opening_copies():
        copy.wait_recv()

    z_side = (jnp.where(gy == 0, EDGE_Z, 0.0), jnp.where(gy == n_gy - 1, EDGE_Z, 0.0))
    z_end = (jnp.where(gx == 0, EDGE_Z, 0.0), jnp.where(gx == n_gx - 1, EDGE_Z, 0.0))
    z_lane = jnp.where(lane16 == 0, z_end[0], 0.0), jnp.where(lane16 == COLS - 1, z_end[1], 0.0)

    for side in range(2):
        step_y = -1.0 if side == 0 else 1.0
        corner_l, corner_r = cbrecv[side * 2], cbrecv[side * 2 + 1]
        for k in PASS1:
            h = rowrecv0[side, k]
            if k == Y:
                h = h + step_y
            if k == Z:
                h = h + z_side[side]
            cl = pltpu.roll(corner_l, (COLS - 2 * k) % COLS, 1)
            cr = pltpu.roll(corner_r, (COLS - 1 - (2 * k + 1)) % COLS, 1)
            if k == Y:
                cl, cr = cl + step_y, cr + step_y
            if k == Z:
                cl, cr = cl + z_side[side], cr + z_side[side]
            hl = jnp.where(lane16 == 0, cl, pltpu.roll(h, 1, 1))
            hr = jnp.where(lane16 == COLS - 1, cr, pltpu.roll(h, COLS - 1, 1))
            if k == X:
                hl, hr = hl - 1.0, hr + 1.0
            if k == Z:
                hl, hr = hl + z_lane[0], hr + z_lane[1]
            rowfar[side * 3, k] = hl
            rowfar[side * 3 + 1, k] = h
            rowfar[side * 3 + 2, k] = hr
        for k in range(VX, VZ + 1):
            h = rowrecv0[side, k]
            cl = pltpu.roll(corner_l, (COLS - 2 * k) % COLS, 1)
            cr = pltpu.roll(corner_r, (COLS - 1 - (2 * k + 1)) % COLS, 1)
            rowfar[side * 3, k] = jnp.where(lane16 == 0, cl, pltpu.roll(h, 1, 1))
            rowfar[side * 3 + 1, k] = h
            rowfar[side * 3 + 2, k] = jnp.where(lane16 == COLS - 1, cr, pltpu.roll(h, COLS - 1, 1))

    for side in range(2):
        for k in range(QUANTITIES):
            colown[side, k] = gather(colsend0[k], own_index[side])
            for h in range(2):
                v = gather(colrecv0[side, k], far_index[side][h])
                if k == X:
                    v = v + (-1.0 if side == 0 else 1.0)
                if k == Z:
                    v = v + z_end[side]
                before, after = pltpu.roll(v, 1, 0), pltpu.roll(v, ROWS - 1, 0)
                if k == Y:
                    before, after = before - 1.0, after + 1.0
                if k == Z:
                    before = jnp.where(row == 0, OUTSIDE_Z, before)
                    after = jnp.where(row == ROWS - 1, OUTSIDE_Z, after)
                for number, value in enumerate((before, v, after)):
                    colfar[side * 6 + number * 2 + h, k] = value

    def halves(ref_at):
        return [ref_at(pl.ds(a * 8, 8)) for a in range(2)]

    def scatter_rows(target, c, side, total):
        target[c, edge_row(side), :] = target[c, edge_row(side), :] + total

    def group_sum(v):
        v = v + pltpu.roll(v, COLS - 1, 1)
        v = v + pltpu.roll(v, COLS - 2, 1)
        return v + pltpu.roll(v, COLS - 4, 1)

    ends = (lane == 0) | (lane == COLS - 1)

    def scatter_columns(target, c, total_l, total_r):
        u = jnp.where((lane & 7) == 0, group_sum(total_l), 0.0)
        u = jnp.where((lane & 7) == 7, pltpu.roll(group_sum(total_r), COLS - 1, 1), u)
        for p in range(SLOTS):
            target[c, at(p), :] += jnp.where(ends, pltpu.roll(u, (COLS - 8 * p) % COLS, 1), 0.0)

    for side in range(2):

        def first_row(number, totals):
            c = side * 3 + number
            t, r = list(totals[:2]), list(totals[2:])
            mine = [[rowsend0[side, k, pl.ds(a * 8, 8), :] for k in PASS1] for a in range(2)]
            for q in range(SLOTS):
                other = [rowfar[c, k, pl.ds(q, 1), :] for k in PASS1]
                for a in range(2):
                    terms = pair_terms(mine[a], other)
                    put(ROW_AT + (c * 16 + q) * 2 + a, terms)
                    t[a] = t[a] + terms[CO] * (other[F] - mine[a][F])
                    r[a] = r[a] + terms[KE] * other[M]
            return (*t, *r)

        t0, t1, r0, r1 = lax.fori_loop(0, 3, first_row, (zero, zero, zero, zero))
        scatter_rows(acc, 0, side, jnp.concatenate([t0, t1], axis=0))
        scatter_rows(acc, 1, side, jnp.concatenate([r0, r1], axis=0))

    column_totals = []
    for side in range(2):
        mine = [colown[side, k] for k in PASS1]

        def first_column(number, totals):
            c = side * 6 + number
            other = [colfar[c, k] for k in PASS1]
            terms = pair_terms(mine, other)
            put(COL_AT + c, terms)
            return totals[0] + terms[CO] * (other[F] - mine[F]), totals[1] + terms[KE] * other[M]

        column_totals.append(lax.fori_loop(0, 6, first_column, (zero, zero)))
    for c in range(2):
        scatter_columns(acc, c, column_totals[0][c], column_totals[1][c])

    best = msrc[3]
    for shift in (4, 2, 1):
        best = jnp.maximum(best, pltpu.roll(best, shift, 0))
    for shift in (64, 32, 16, 8, 4, 2, 1):
        best = jnp.maximum(best, pltpu.roll(best, shift, 1))
    step_dt = COURANT / best

    def total_of(target, per_dir, c, p):
        return target[c, at(p), :] + unshifted(*(per_dir[d, c, p] for d in range(4)))

    first_weight, coefs = rkl_table(SECTIONS)

    def first_update(p, carry):
        live = p < pop[...]
        start = own[F, at(p), :]
        lap = jnp.where(live, total_of(acc, accj, 0, p) / cap[p], 0.0) * step_dt
        m = own[M, at(p), :]
        density = jnp.where(live, m + total_of(acc, accj, 1, p), 1.0)
        inverse = 1.0 / density
        lap0[p] = lap
        y = start + first_weight * lap
        ycur[at(p), :] = y
        yprev[p] = start
        gfac[0, at(p), :] = ROOT_HALF * m * inverse
        press[1, at(p), :] = 6.0 * (HEAT_RATIO - 1.0) * inverse
        for d, v in enumerate(shifted(y)):
            sfar[0, d, p] = v
        for d, v in enumerate(shifted(gfac[0, at(p), :])):
            sfar[1, d, p] = v
        acc[0, at(p), :] = zero
        for d in range(4):
            accj[d, 0, p] = zero
        return carry

    lax.fori_loop(0, SLOTS, first_update, 0)

    def send(e, sources):
        first, count = EXCHANGES[e - 1]
        for n in range(count):
            tile, edge = sources[n]
            for side in range(2):
                rsend[side, first + n] = edge(side)
            vsend[first + n] = packed_columns(tile)
        for copy in section_copies(e):
            copy.start()

    def receive(e):
        for copy in section_copies(e):
            copy.wait_recv()
        first, count = EXCHANGES[e - 1]
        for n in range(first, first + count):
            for side in range(2):
                h = rrecv[side, n]
                hl, hr = drecv[side * 2, n], drecv[side * 2 + 1, n]
                hs[n, side * 3] = pltpu.roll(jnp.where(lane16 == COLS - 1, hl, h), 1, 1)
                hs[n, side * 3 + 1] = h
                hs[n, side * 3 + 2] = pltpu.roll(jnp.where(lane16 == 0, hr, h), COLS - 1, 1)
                oc[n, side] = gather(vsend[n], own_index[side])
                for half in range(2):
                    v = gather(vrecv[side, n], far_index[side][half])
                    for number, value in enumerate((pltpu.roll(v, 1, 0), v, pltpu.roll(v, ROWS - 1, 0))):
                        cf[n, side * 6 + number * 2 + half] = value

    def flat_source(ref):
        return (lambda p: ref[at(p), :]), (lambda side: ref[edge_row(side), :])

    def section_dirs(n, carry):
        d = lax.div(n, 4)
        p0 = lax.rem(n, 4) * 4
        mine = [ycur[at(p0 + a), :] for a in range(4)]
        ti = [zero] * 4
        for q in range(SLOTS):
            other = sfar[0, d, q]
            tj = None
            for a in range(4):
                t = store[CO, d * 256 + (p0 + a) * 16 + q] * (other - mine[a])
                ti[a] = ti[a] + t
                tj = t if tj is None else tj + t
            accj[d, 0, q] = accj[d, 0, q] - tj
        for a in range(4):
            acc[0, at(p0 + a), :] += ti[a]
        return carry

    def section_self_some(steps):
        def section_self(p, carry):
            mine = ycur[at(p), :]
            ti = zero
            for step in steps:
                q = lax.rem(p + step, SLOTS)
                t = store[CO, SELF_AT + p * 8 + (step - 1)] * (ycur[at(q), :] - mine)
                ti = ti + t
                acc[0, at(q), :] += -t
            acc[0, at(p), :] += ti
            return carry

        return section_self

    def section_inside():
        lax.fori_loop(0, 16, section_dirs, 0)
        lax.fori_loop(0, SLOTS, section_self_some(range(1, 8)), 0)
        lax.fori_loop(0, SLOTS // 2, section_self_some((8,)), 0)

    def section_outside(n):
        for side in range(2):
            mine = [rsend[side, n, pl.ds(a * 8, 8), :] for a in range(2)]
            t = [zero, zero]
            for number in range(3):
                c = side * 3 + number
                for q in range(SLOTS):
                    other = hs[n, c, pl.ds(q, 1), :]
                    for a in range(2):
                        t[a] = t[a] + store[CO, ROW_AT + (c * 16 + q) * 2 + a] * (other - mine[a])
            scatter_rows(acc, 0, side, jnp.concatenate(t, axis=0))
        totals = []
        for side in range(2):
            mine = oc[n, side]
            t = zero
            for number in range(6):
                c = side * 6 + number
                t = t + store[CO, COL_AT + c] * (cf[n, c] - mine)
            totals.append(t)
        scatter_columns(acc, 0, *totals)

    def section_update(coef, last):
        m, n, weight, gamma = coef

        def update(p, carry):
            live = p < pop[...]
            start = own[F, at(p), :]
            lap = jnp.where(live, total_of(acc, accj, 0, p) / cap[p], 0.0) * step_dt
            now = ycur[at(p), :]
            y = m * now + n * yprev[p] + (1.0 - m - n) * start + weight * lap + gamma * lap0[p]
            if last:
                heated[p] = y
                pr = press[1, at(p), :] * y
                press[0, at(p), :] = pr
                for d, v in enumerate(shifted(pr)):
                    sfar[0, d, p] = v
            else:
                yprev[p] = now
                ycur[at(p), :] = y
                for d, v in enumerate(shifted(y)):
                    sfar[0, d, p] = v
                acc[0, at(p), :] = zero
                for d in range(4):
                    accj[d, 0, p] = zero
            return carry

        lax.fori_loop(0, SLOTS, update, 0)

    def drag_dirs(n, carry):
        d = lax.div(n, 8)
        p0 = lax.rem(n, 8) * 2
        g = [gfac[0, at(p0 + a), :] for a in range(2)]
        v = [[own[VX + c, at(p0 + a), :] for c in range(3)] for a in range(2)]
        total = [[zero] * 3 for _ in range(2)]
        for q in range(SLOTS):
            gj = sfar[1, d, q]
            vj = [far[d, VX + c, q] for c in range(3)]
            back = [None] * 3
            for a in range(2):
                w = store[KE, d * 256 + (p0 + a) * 16 + q] * (g[a] * gj)
                for c in range(3):
                    e = w * (vj[c] - v[a][c])
                    total[a][c] = total[a][c] + e
                    back[c] = e if back[c] is None else back[c] + e
            for c in range(3):
                kaccj[d, c, q] = kaccj[d, c, q] - back[c]
        for a in range(2):
            for c in range(3):
                kacc[c, at(p0 + a), :] += total[a][c]
        return carry

    def drag_self_some(steps):
        def drag_self(p, carry):
            g = gfac[0, at(p), :]
            v = [own[VX + c, at(p), :] for c in range(3)]
            total = [zero] * 3
            for step in steps:
                q = lax.rem(p + step, SLOTS)
                w = store[KE, SELF_AT + p * 8 + (step - 1)] * (g * gfac[0, at(q), :])
                for c in range(3):
                    e = w * (own[VX + c, at(q), :] - v[c])
                    total[c] = total[c] + e
                    kacc[c, at(q), :] += -e
            for c in range(3):
                kacc[c, at(p), :] += total[c]
            return carry

        return drag_self

    def drag_outside():
        for side in range(2):
            g = [rsend[side, EX_G, pl.ds(a * 8, 8), :] for a in range(2)]
            v = [[rowsend0[side, VX + c, pl.ds(a * 8, 8), :] for c in range(3)] for a in range(2)]

            def one(number, totals):
                c = side * 3 + number
                total = list(totals)
                for q in range(SLOTS):
                    gj = hs[EX_G, c, pl.ds(q, 1), :]
                    vj = [rowfar[c, VX + x, pl.ds(q, 1), :] for x in range(3)]
                    for a in range(2):
                        w = store[KE, ROW_AT + (c * 16 + q) * 2 + a] * (g[a] * gj)
                        for x in range(3):
                            total[a * 3 + x] = total[a * 3 + x] + w * (vj[x] - v[a][x])
                return tuple(total)

            total = lax.fori_loop(0, 3, one, (zero,) * 6)
            for x in range(3):
                scatter_rows(kacc, x, side, jnp.concatenate([total[x], total[3 + x]], axis=0))
        totals = []
        for side in range(2):
            total = [zero] * 3
            for number in range(6):
                c = side * 6 + number
                w = store[KE, COL_AT + c] * (oc[EX_G, side] * cf[EX_G, c])
                for x in range(3):
                    total[x] = total[x] + w * (colfar[c, VX + x] - colown[side, VX + x])
            totals.append(total)
        for x in range(3):
            scatter_columns(kacc, x, totals[0][x], totals[1][x])

    def push_dirs(n, carry):
        d = lax.div(n, 8)
        p0 = lax.rem(n, 8) * 2
        pi = [press[0, at(p0 + a), :] for a in range(2)]
        total = [[zero] * 3 for _ in range(2)]
        for q in range(SLOTS):
            pj = sfar[0, d, q]
            back = [None] * 3
            for a in range(2):
                both = pi[a] + pj
                for c in range(3):
                    e = both * store[WX + c, d * 256 + (p0 + a) * 16 + q]
                    total[a][c] = total[a][c] + e
                    back[c] = e if back[c] is None else back[c] + e
            for c in range(3):
                kaccj[d, c, q] = kaccj[d, c, q] - back[c]
        for a in range(2):
            for c in range(3):
                kacc[c, at(p0 + a), :] += total[a][c]
        return carry

    def push_self_some(steps):
        def push_self(p, carry):
            pi = press[0, at(p), :]
            total = [zero] * 3
            for step in steps:
                q = lax.rem(p + step, SLOTS)
                both = pi + press[0, at(q), :]
                for c in range(3):
                    e = both * store[WX + c, SELF_AT + p * 8 + (step - 1)]
                    total[c] = total[c] + e
                    kacc[c, at(q), :] += -e
            for c in range(3):
                kacc[c, at(p), :] += total[c]
            return carry

        return push_self

    def push_outside():
        for side in range(2):
            pi = [rsend[side, EX_P, pl.ds(a * 8, 8), :] for a in range(2)]

            def one(number, totals):
                c = side * 3 + number
                total = list(totals)
                for q in range(SLOTS):
                    pj = hs[EX_P, c, pl.ds(q, 1), :]
                    for a in range(2):
                        both = pi[a] + pj
                        for x in range(3):
                            total[a * 3 + x] = (
                                total[a * 3 + x] + both * store[WX + x, ROW_AT + (c * 16 + q) * 2 + a]
                            )
                return tuple(total)

            total = lax.fori_loop(0, 3, one, (zero,) * 6)
            for x in range(3):
                scatter_rows(kacc, x, side, jnp.concatenate([total[x], total[3 + x]], axis=0))
        totals = []
        for side in range(2):
            total = [zero] * 3
            for number in range(6):
                c = side * 6 + number
                both = oc[EX_P, side] + cf[EX_P, c]
                for x in range(3):
                    total[x] = total[x] + both * store[WX + x, COL_AT + c]
            totals.append(total)
        for x in range(3):
            scatter_columns(kacc, x, totals[0][x], totals[1][x])

    send(1, [flat_source(ycur), flat_source(gfac.at[0])])
    section_inside()
    lax.fori_loop(0, SLOTS, drag_self_some(range(1, 8)), 0)
    lax.fori_loop(0, SLOTS // 2, drag_self_some((8,)), 0)
    lax.fori_loop(0, 8, drag_dirs, 0)
    receive(1)
    section_outside(EX_Y1)
    section_update(coefs[0], False)

    send(2, [flat_source(ycur)])
    section_inside()
    lax.fori_loop(8, 20, drag_dirs, 0)
    receive(2)
    section_outside(EX_Y2)
    section_update(coefs[1], False)

    send(3, [flat_source(ycur)])
    section_inside()
    lax.fori_loop(20, 32, drag_dirs, 0)
    drag_outside()
    receive(3)
    section_outside(EX_Y3)
    section_update(coefs[2], True)

    send(4, [flat_source(press.at[0])])
    lax.fori_loop(0, 32, push_dirs, 0)
    lax.fori_loop(0, SLOTS, push_self_some(range(1, 8)), 0)
    lax.fori_loop(0, SLOTS // 2, push_self_some((8,)), 0)
    receive(4)
    push_outside()

    def finish(p, carry):
        live = p < pop[...]
        scale = jnp.where(live, step_dt / own[M, at(p), :], 0.0)
        for c in range(3):
            moved[c, p] = own[VX + c, at(p), :] + scale * total_of(kacc, kaccj, c, p)
        return carry

    lax.fori_loop(0, SLOTS, finish, 0)

    for copy in opening_copies():
        copy.wait_send()
    for e in range(1, 5):
        for copy in section_copies(e):
            copy.wait_send()
    for stage in range(3):
        for copy in stage_copies(stage):
            copy.wait_send()


def body(sizes, *args):
    f32 = jnp.float32
    messages = sum(sizes) - 3
    tile = (SLOTS, ROWS, COLS)
    vmem = pl.BlockSpec(memory_space=pltpu.VMEM)
    scratch = [
        pltpu.VMEM((QUANTITIES, FLAT, COLS), f32),
        pltpu.VMEM((4, QUANTITIES) + tile, f32),
        pltpu.VMEM((FLAT, COLS), f32),
        pltpu.VMEM(tile, f32),
        pltpu.VMEM(tile, f32),
        pltpu.VMEM((1, FLAT, COLS), f32),
        pltpu.VMEM((2, FLAT, COLS), f32),
        pltpu.VMEM((2, 4) + tile, f32),
        pltpu.VMEM((2, FLAT, COLS), f32),
        pltpu.VMEM((4, 2) + tile, f32),
        pltpu.VMEM((3, FLAT, COLS), f32),
        pltpu.VMEM((4, 3) + tile, f32),
        pltpu.VMEM((5, PAIRS, ROWS, COLS), f32),
        pltpu.VMEM((2, QUANTITIES, SLOTS, COLS), f32),
        pltpu.VMEM((2, QUANTITIES, SLOTS, COLS), f32),
        pltpu.VMEM((QUANTITIES, ROWS, COLS), f32),
        pltpu.VMEM((2, QUANTITIES, ROWS, COLS), f32),
        pltpu.VMEM((2, SLOTS, COLS), f32),
        pltpu.VMEM((4, SLOTS, COLS), f32),
        pltpu.VMEM((6, QUANTITIES, SLOTS, COLS), f32),
        pltpu.VMEM((12, QUANTITIES, ROWS, COLS), f32),
        pltpu.VMEM((2, QUANTITIES, ROWS, COLS), f32),
        pltpu.VMEM((2, 5, SLOTS, COLS), f32),
        pltpu.VMEM((2, 5, SLOTS, COLS), f32),
        pltpu.VMEM((5, ROWS, COLS), f32),
        pltpu.VMEM((2, 5, ROWS, COLS), f32),
        pltpu.VMEM((4, 5, SLOTS, COLS), f32),
        pltpu.VMEM((5, 6, SLOTS, COLS), f32),
        pltpu.VMEM((5, 12, ROWS, COLS), f32),
        pltpu.VMEM((5, 2, ROWS, COLS), f32),
        pltpu.VMEM((4, ROWS, COLS), f32),
        pltpu.VMEM((messages, ROWS, COLS), f32),
        pltpu.SemaphoreType.DMA((5, 8)),
        pltpu.SemaphoreType.DMA((5, 8)),
        pltpu.SemaphoreType.DMA((messages,)),
        pltpu.SemaphoreType.DMA((messages,)),
    ]
    return pl.pallas_call(
        functools.partial(kernel, sizes),
        out_shape=(jax.ShapeDtypeStruct(tile, f32), jax.ShapeDtypeStruct((3,) + tile, f32)),
        in_specs=[vmem] * 8,
        out_specs=(vmem, vmem),
        scratch_shapes=scratch,
        compiler_params=pltpu.CompilerParams(
            collective_id=0, has_side_effects=True, vmem_limit_bytes=52 * 1024 * 1024
        ),
        name="sections_and_kick",
    )(*args)


def solution(mesh):
    n_gx, n_gy = mesh.shape["gx"], mesh.shape["gy"]
    n_hi = 4 if n_gy % 4 == 0 and n_gy > 4 else 2
    sizes = (n_gx, n_gy // n_hi, n_hi)
    cells = P("gy", "gx")
    one = P(None, "gy", "gx")
    many = P(None, None, "gy", "gx")
    return jax.shard_map(
        functools.partial(body, sizes),
        mesh=mesh,
        in_specs=(cells, many, many, one, one, one, one, many),
        out_specs=(one, many),
        check_vma=False,
    )
```

profile of v0, /device:TPU:1, one launch (start us, length us, event | category | flops | bytes accessed | tf_op | source)
XLA Modules:
  0.0 67.0 jit_solution(772623281001243046)
XLA Ops:
  0.6 0.0 copy-start
  0.6 0.9 %copy-done = f32[3,16,8,128]{3,2,1,0:T(8,128)S(1)} copy-done((f32[3,16,8,128]{3,2,1,0:T(8,128)S(1)}, f32[3,16,8,128]{3,2,1,0:T(8,128)}, u32[]{:S(2)}) %copy-start) | copy-done | bytes 196632
  1.6 0.0 copy-start.1
  1.6 0.9 %copy-done.1 = f32[3,16,8,128]{3,2,1,0:T(8,128)S(1)} copy-done((f32[3,16,8,128]{3,2,1,0:T(8,128)S(1)}, f32[3,16,8,128]{3,2,1,0:T(8,128)}, u32[]{:S(2)}) %copy-start.1) | copy-done | bytes 196632
  2.5 0.0 copy-start.2
  2.5 0.9 %copy-done.2 = f32[2,16,8,128]{3,2,1,0:T(8,128)S(1)} copy-done((f32[2,16,8,128]{3,2,1,0:T(8,128)S(1)}, f32[2,16,8,128]{3,2,1,0:T(8,128)}, u32[]{:S(2)}) %copy-start.2) | copy-done | bytes 131096
  3.4 0.0 copy-start.3
  3.4 0.8 %copy-done.3 = f32[16,8,128]{2,1,0:T(8,128)S(1)} copy-done((f32[16,8,128]{2,1,0:T(8,128)S(1)}, f32[16,8,128]{2,1,0:T(8,128)}, u32[]{:S(2)}) %copy-start.3) | copy-done | bytes 65560
  4.2 0.0 copy-start.4
  4.2 0.8 %copy-done.4 = f32[16,8,128]{2,1,0:T(8,128)S(1)} copy-done((f32[16,8,128]{2,1,0:T(8,128)S(1)}, f32[16,8,128]{2,1,0:T(8,128)}, u32[]{:S(2)}) %copy-start.4) | copy-done | bytes 65560
  5.1 0.0 copy-start.5
  5.1 0.8 %copy-done.5 = f32[16,8,128]{2,1,0:T(8,128)S(1)} copy-done((f32[16,8,128]{2,1,0:T(8,128)S(1)}, f32[16,8,128]{2,1,0:T(8,128)}, u32[]{:S(2)}) %copy-start.5) | copy-done | bytes 65560
  5.9 0.0 copy-start.6
  5.9 0.8 %copy-done.6 = f32[16,8,128]{2,1,0:T(8,128)S(1)} copy-done((f32[16,8,128]{2,1,0:T(8,128)S(1)}, f32[16,8,128]{2,1,0:T(8,128)}, u32[]{:S(2)}) %copy-start.6) | copy-done | bytes 65560
  6.8 0.0 copy-start.7
  6.8 0.7 %copy-done.7 = s32[8,128]{1,0:T(8,128)S(1)} copy-done((s32[8,128]{1,0:T(8,128)S(1)}, s32[8,128]{1,0:T(8,128)}, u32[]{:S(2)}) %copy-start.7) | copy-done | bytes 4120
  7.4 58.3 %sections_and_kick.1 = (f32[16,8,128]{2,1,0:T(8,128)S(1)}, f32[3,16,8,128]{3,2,1,0:T(8,128)S(1)}) custom-call(s32[8,128]{1,0:T(8,128)S(1)} %copy-done.7, f32[3,16,8,128]{3,2,1,0:T(8,128)S(1)} %copy-done, f32[2,16,8,128]{3,2,1,0:T(8,128)S(1)} %copy-done.2, f32[16,8,128]{2,1,0:T(8,128)S(1)} %copy-done.3, f32[16,8,128]{2,1,0:T(8,128)S(1)} %copy-done.4, ...), custom_call_target="tpu_custom_call" | custom-call | tf_op jit(solution)/shard_map/sections_and_kick/pallas_call | solution.py:886
  65.7 0.6 copy.12
  66.3 0.7 %copy.13 = f32[3,16,8,128]{3,2,1,0:T(8,128)} copy(f32[3,16,8,128]{3,2,1,0:T(8,128)S(1)} %get-tuple-element.5) | data formatting | bytes 393216
Async XLA Ops:
  0.6 0.9 %copy-start = (f32[3,16,8,128]{3,2,1,0:T(8,128)S(1)}, f32[3,16,8,128]{3,2,1,0:T(8,128)}, u32[]{:S(2)}) copy-start(f32[3,16,8,128]{3,2,1,0:T(8,128)} %loc.1) | copy-start | bytes 589828
  1.6 0.9 %copy-start.1 = (f32[3,16,8,128]{3,2,1,0:T(8,128)S(1)}, f32[3,16,8,128]{3,2,1,0:T(8,128)}, u32[]{:S(2)}) copy-start(f32[3,16,8,128]{3,2,1,0:T(8,128)} %mot.1) | copy-start | bytes 589828
  2.5 0.9 %copy-start.2 = (f32[2,16,8,128]{3,2,1,0:T(8,128)S(1)}, f32[2,16,8,128]{3,2,1,0:T(8,128)}, u32[]{:S(2)}) copy-start(f32[2,16,8,128]{3,2,1,0:T(8,128)} %tilt.1) | copy-start | bytes 393220
  3.4 0.8 %copy-start.3 = (f32[16,8,128]{2,1,0:T(8,128)S(1)}, f32[16,8,128]{2,1,0:T(8,128)}, u32[]{:S(2)}) copy-start(f32[16,8,128]{2,1,0:T(8,128)} %mass.1) | copy-start | bytes 196612
  4.2 0.8 %copy-start.4 = (f32[16,8,128]{2,1,0:T(8,128)S(1)}, f32[16,8,128]{2,1,0:T(8,128)}, u32[]{:S(2)}) copy-start(f32[16,8,128]{2,1,0:T(8,128)} %kappa.1) | copy-start | bytes 196612
  5.1 0.8 %copy-start.5 = (f32[16,8,128]{2,1,0:T(8,128)S(1)}, f32[16,8,128]{2,1,0:T(8,128)}, u32[]{:S(2)}) copy-start(f32[16,8,128]{2,1,0:T(8,128)} %cap.1) | copy-start | bytes 196612
  5.9 0.8 %copy-start.6 = (f32[16,8,128]{2,1,0:T(8,128)S(1)}, f32[16,8,128]{2,1,0:T(8,128)}, u32[]{:S(2)}) copy-start(f32[16,8,128]{2,1,0:T(8,128)} %temp.1) | copy-start | bytes 196612
  6.8 0.7 %copy-start.7 = (s32[8,128]{1,0:T(8,128)S(1)}, s32[8,128]{1,0:T(8,128)}, u32[]{:S(2)}) copy-start(s32[8,128]{1,0:T(8,128)} %pop.1) | copy-start | bytes 12292
where the time goes:
time: 67.4 us; the launch traced here: 67 us
  Pallas kernels  58.3 us (86%)
  local copies, waits for them, and re-layouts  8.1 us (12%)
    pallas_call x1, Pallas kernels, body(): pl.pallas_call(functools.partial(kernel, sizes), out_shape=(jax.ShapeDtyp...  58.3 us
    unnamed x18, local copies, waits for them, and re-layouts  8.1 us

commit v1 on v0

v1 whole, which is shorter than its diff:
```python
import functools

import jax
import jax.numpy as jnp
from jax import lax
from jax.experimental import pallas as pl
from jax.experimental.pallas import tpu as pltpu
from jax.sharding import PartitionSpec as P

SECTIONS = 4
ISO_PART = 0.1
HEAT_RATIO = 5.0 / 3.0
COURANT = 0.3
ROOT_HALF = 0.5**0.5
MESH = pl.DeviceIdType.MESH

SLOTS = 16
ROWS = 8
COLS = 128
FLAT = SLOTS * ROWS

X, Y, Z, BX, BY, BZ, KA, F, M, VX, VY, VZ = range(12)
QUANTITIES = 12

DIRS = ((0, 1), (1, -1), (1, 0), (1, 1))

CO, KE, WX, WY, WZ = range(5)
SELF_AT = len(DIRS) * SLOTS * SLOTS
ROW_AT = SELF_AT + SLOTS * 8
COL_AT = ROW_AT + 6 * SLOTS * 2
PAIRS = COL_AT + 12

ROUNDS = 4
FIELD, DRAG = range(2)

EMPTY_Z = 10.0
OUTSIDE_Z = 20.0
EDGE_Z = 40.0

SIN = (0.9999999957157406, -0.1666665796974384, 0.008333050613415454, -0.0001980904606136566, 2.605165590448684e-06)
COS = (
    0.9999999997798981,
    -0.4999999935694129,
    0.04166663620835954,
    -0.001388836083517328,
    2.476013513307355e-05,
    -2.605106944029617e-07,
)


def section_polynomial(section_total):
    weight = 4.0 / (section_total * section_total + section_total - 2)
    series = [1.0 / 3.0, 1.0 / 3.0, 1.0 / 3.0]
    for j in range(3, section_total + 1):
        series.append((j * j + j - 2) / (2.0 * j * (j + 1)))

    def padded(values):
        return values + [0.0] * (section_total + 1 - len(values))

    before, now = padded([1.0]), padded([1.0, series[1] * weight])
    for j in range(2, section_total + 1):
        m = (2 * j - 1) / j * series[j] / series[j - 1]
        n = -(j - 1) / j * series[j] / series[j - 2]
        after = [m * a + n * b for a, b in zip(now, before)]
        after[0] += 1.0 - m - n
        after[1] -= (1.0 - series[j - 1]) * m * weight
        for k in range(section_total):
            after[k + 1] += m * weight * now[k]
        before, now = now, after
    return now


def horner(coefs, t):
    total = jnp.full_like(t, coefs[-1])
    for c in coefs[-2::-1]:
        total = total * t + c
    return total


def sin_cos(angle):
    half = 0.5 * angle
    t = half * half
    s = half * horner(SIN, t)
    c = horner(COS, t)
    return 2.0 * s * c, 1.0 - 2.0 * s * s


def pair_terms(i, j):
    dx, dy, dz = i[X] - j[X], i[Y] - j[Y], i[Z] - j[Z]
    s = jnp.maximum(1.0 - (dx * dx + dy * dy + dz * dz), 0.0)
    s2 = s * s
    own = i[BX] * dx + i[BY] * dy + i[BZ] * dz
    far = j[BX] * dx + j[BY] * dy + j[BZ] * dz
    co = (s2 * s) * (ISO_PART + (own * own + far * far)) * (i[KA] + j[KA])
    w = s2 * (i[M] * j[M])
    return co, w * s, w * dx, w * dy, w * dz


def kernel(
    sizes,
    pop_in,
    loc_in,
    tilt_in,
    mass_in,
    kappa_in,
    cap_in,
    temp_in,
    mot_in,
    heated,
    moved,
    pop,
    loc,
    tilt,
    mass,
    kappa,
    cap,
    temp,
    mot,
    own,
    far,
    field,
    powers,
    gfac,
    pfac,
    sfar,
    gfar,
    acc,
    accj,
    kacc,
    kaccj,
    store,
    rowsend0,
    rowrecv0,
    colsend0,
    colrecv0,
    cbsend,
    cbrecv,
    rowfar,
    colfar,
    colown,
    coltot,
    rsend,
    rrecv,
    vsend,
    vrecv,
    drecv,
    hs,
    cf,
    oc,
    msrc,
    mrecv,
    send_sem,
    recv_sem,
    msend_sem,
    mrecv_sem,
    load_sem,
):
    loads = [
        pltpu.make_async_copy(src, dst, load_sem.at[number])
        for number, (src, dst) in enumerate(
            (
                (pop_in, pop),
                (loc_in, loc),
                (tilt_in, tilt),
                (mass_in, mass),
                (kappa_in, kappa),
                (cap_in, cap),
                (temp_in, temp),
                (mot_in, mot),
            )
        )
    ]
    for load in loads:
        load.start()

    n_gx, n_lo, n_hi = sizes
    n_gy = n_lo * n_hi
    gx = lax.axis_index("gx")
    gy = lax.axis_index("gy")
    left, right = lax.rem(gx + n_gx - 1, n_gx), lax.rem(gx + 1, n_gx)
    up, down = lax.rem(gy + n_gy - 1, n_gy), lax.rem(gy + 1, n_gy)
    lo, hi = lax.rem(gy, n_lo), lax.div(gy, n_lo)

    around = ((gx, up), (gx, down), (left, gy), (right, gy), (left, up), (right, up), (left, down), (right, down))

    stage_size = (n_gx - 1, n_lo - 1, n_hi - 1)
    stage_at = (0, n_gx - 1, n_gx + n_lo - 2)

    def stage_device(stage, k):
        if stage == 0:
            return (lax.rem(gx + k + 1, n_gx), gy)
        if stage == 1:
            return (gx, hi * n_lo + lax.rem(lo + k + 1, n_lo))
        return (gx, lax.rem(hi + k + 1, n_hi) * n_lo + lo)

    def each(count, fn):
        def run(k, carry):
            fn(k)
            return carry

        lax.fori_loop(0, count, run, 0)

    barrier = pltpu.get_barrier_semaphore()

    def greet(device):
        pl.semaphore_signal(barrier, inc=1, device_id=device, device_id_type=MESH)

    for device in around:
        greet(device)
    for stage in range(3):
        each(stage_size[stage], lambda k, stage=stage: greet(stage_device(stage, k)))

    lane = lax.broadcasted_iota(jnp.int32, (ROWS, COLS), 1)
    row = lax.broadcasted_iota(jnp.int32, (ROWS, COLS), 0)
    lane16 = lax.broadcasted_iota(jnp.int32, (SLOTS, COLS), 1)
    zero = jnp.zeros((ROWS, COLS), jnp.float32)

    def at(p):
        start = p * ROWS
        return pl.ds(start if isinstance(p, int) else pl.multiple_of(start, ROWS), ROWS)

    def edge_row(side):
        return pl.ds(side * (ROWS - 1), SLOTS, stride=ROWS)

    def half(a):
        return pl.ds(a * 8, 8)

    def shifted(v):
        low = pltpu.roll(v, ROWS - 1, 0)
        return (pltpu.roll(v, COLS - 1, 1), pltpu.roll(low, 1, 1), low, pltpu.roll(low, COLS - 1, 1))

    def unshifted(a, b, c, d):
        return pltpu.roll(a, 1, 1) + pltpu.roll(pltpu.roll(b, COLS - 1, 1) + c + pltpu.roll(d, 1, 1), 1, 0)

    def gather(v, index):
        return jnp.take_along_axis(v, index, axis=1)

    def packed_columns(tile_of):
        v = tile_of(0)
        for p in range(1, SLOTS):
            mask = (lane == 8 * p) | (lane == 8 * p - 1)
            v = jnp.where(mask, pltpu.roll(tile_of(p), 8 * p, 1), v)
        return v

    group = lane & ~7
    within = (lane & 7) * 8
    own_index = (group, (group + (COLS - 1)) & (COLS - 1))
    far_index = (
        ((within + (COLS - 1)) & (COLS - 1), (within + 63) & (COLS - 1)),
        (within, within + 64),
    )

    def prepare(p, fastest):
        live = p < pop[...]
        sin_p, cos_p = sin_cos(tilt[0, p])
        sin_a, cos_a = sin_cos(tilt[1, p])
        t = temp[p]
        v = [mot[c, p] for c in range(3)]
        values = [
            loc[0, p],
            loc[1, p],
            jnp.where(live, loc[2, p], EMPTY_Z),
            ROOT_HALF * (sin_p * cos_a),
            ROOT_HALF * (sin_p * sin_a),
            ROOT_HALF * cos_p,
            0.5 * kappa[p],
            t,
            mass[p],
        ] + v
        for k in range(QUANTITIES):
            own[k, at(p), :] = values[k]
        for c in range(2):
            acc[c, at(p), :] = zero
        for c in range(3):
            kacc[c, at(p), :] = zero
        speed = jnp.sqrt(HEAT_RATIO * (HEAT_RATIO - 1.0) * t) + jnp.sqrt(v[0] * v[0] + v[1] * v[1] + v[2] * v[2])
        return jnp.maximum(fastest, jnp.where(live, speed, 0.0))

    for load in loads:
        load.wait()
    msrc[0] = lax.fori_loop(0, SLOTS, prepare, zero)

    def pack(k, cb):
        cb = list(cb)
        for side in range(2):
            packed = own[k, edge_row(side), :]
            rowsend0[side, k] = packed
            mask = (lane16 == 2 * k) | (lane16 == 2 * k + 1)
            cb[side] = jnp.where(mask, pltpu.roll(packed, 2 * k + 1, 1), cb[side])
        colsend0[k] = packed_columns(lambda p: own[k, at(p), :])
        return tuple(cb)

    blank = jnp.zeros((SLOTS, COLS), jnp.float32)
    cbsend[0], cbsend[1] = lax.fori_loop(0, QUANTITIES, pack, (blank, blank))

    def remote(src, dst, s, r, device):
        return pltpu.make_async_remote_copy(
            src_ref=src, dst_ref=dst, send_sem=s, recv_sem=r, device_id=device, device_id_type=MESH
        )

    def stage_copy(stage, k):
        slot = stage_at[stage] + k
        return remote(
            msrc.at[stage], mrecv.at[slot], msend_sem.at[slot], mrecv_sem.at[slot], stage_device(stage, k)
        )

    def stage_start(stage):
        each(stage_size[stage], lambda k: stage_copy(stage, k).start())

    def stage_finish(stage):
        def take(k, best):
            stage_copy(stage, k).wait_recv()
            return jnp.maximum(best, mrecv[stage_at[stage] + k])

        msrc[stage + 1] = lax.fori_loop(0, stage_size[stage], take, msrc[stage])

    def opening_copies():
        plan = (
            (rowsend0.at[0], rowrecv0.at[1]),
            (rowsend0.at[1], rowrecv0.at[0]),
            (colsend0, colrecv0.at[1]),
            (colsend0, colrecv0.at[0]),
            (cbsend.at[0], cbrecv.at[3]),
            (cbsend.at[0], cbrecv.at[2]),
            (cbsend.at[1], cbrecv.at[1]),
            (cbsend.at[1], cbrecv.at[0]),
        )
        return [
            remote(src, dst, send_sem.at[ROUNDS, c], recv_sem.at[ROUNDS, c], around[c])
            for c, (src, dst) in enumerate(plan)
        ]

    def round_copies(e):
        plan = (
            (rsend.at[e, 0], rrecv.at[e, 1]),
            (rsend.at[e, 1], rrecv.at[e, 0]),
            (vsend.at[e], vrecv.at[e, 1]),
            (vsend.at[e], vrecv.at[e, 0]),
            (rsend.at[e, 0], drecv.at[e, 3]),
            (rsend.at[e, 0], drecv.at[e, 2]),
            (rsend.at[e, 1], drecv.at[e, 1]),
            (rsend.at[e, 1], drecv.at[e, 0]),
        )
        return [
            remote(src, dst, send_sem.at[e, c], recv_sem.at[e, c], around[c]) for c, (src, dst) in enumerate(plan)
        ]

    pl.semaphore_wait(barrier, len(around) + sum(stage_size))
    for copy in opening_copies():
        copy.start()
    stage_start(0)

    PASS1 = range(9)

    def put(index, terms):
        for c in range(5):
            store[c, index] = terms[c]

    def first_self(p, carry):
        mine = [own[k, at(p), :] for k in PASS1]
        ti, ri = zero, zero
        for step in range(1, 9):
            q = lax.rem(p + step, SLOTS)
            other = [own[k, at(q), :] for k in PASS1]
            terms = pair_terms(mine, other)
            put(SELF_AT + p * 8 + (step - 1), terms)
            t = terms[CO] * (other[F] - mine[F])
            ti = ti + t
            ri = ri + terms[KE]
            if step < 8:
                acc[0, at(q), :] += -t
                acc[1, at(q), :] += terms[KE]
        acc[0, at(p), :] += ti
        acc[1, at(p), :] += ri
        for k in range(QUANTITIES):
            for d, v in enumerate(shifted(own[k, at(p), :])):
                if k == X and DIRS[d][1]:
                    v = v + float(DIRS[d][1])
                if k == Y and DIRS[d][0]:
                    v = v + float(DIRS[d][0])
                if k == Z:
                    out = None
                    for step, index, last in ((DIRS[d][0], row, ROWS - 1), (DIRS[d][1], lane, COLS - 1)):
                        if step:
                            hit = index == (last if step > 0 else 0)
                            out = hit if out is None else out | hit
                    v = jnp.where(out, OUTSIDE_Z, v)
                far[d, k, p] = v
        for d in range(4):
            for c in range(2):
                accj[d, c, p] = zero
            for c in range(3):
                kaccj[d, c, p] = zero
        return carry

    def first_dirs(n, carry):
        d = lax.div(n, 8)
        p0 = lax.rem(n, 8) * 2
        mine = [[own[k, at(p0 + a), :] for k in PASS1] for a in range(2)]
        ti = [zero, zero]
        ri = [zero, zero]
        for q in range(SLOTS):
            other = [far[d, k, q] for k in PASS1]
            tj, rj = None, None
            for a in range(2):
                terms = pair_terms(mine[a], other)
                put(d * 256 + (p0 + a) * 16 + q, terms)
                t, r = terms[CO] * (other[F] - mine[a][F]), terms[KE]
                ti[a] = ti[a] + t
                ri[a] = ri[a] + r
                tj = t if tj is None else tj + t
                rj = r if rj is None else rj + r
            accj[d, 0, q] = accj[d, 0, q] - tj
            accj[d, 1, q] = accj[d, 1, q] + rj
        for a in range(2):
            acc[0, at(p0 + a), :] += ti[a]
            acc[1, at(p0 + a), :] += ri[a]
        return carry

    lax.fori_loop(0, SLOTS, first_self, 0)
    lax.fori_loop(0, 32, first_dirs, 0)
    stage_finish(0)
    stage_start(1)

    for copy in opening_copies():
        copy.wait_recv()

    def rows_around(k, carry):
        for side in range(2):
            h = rowrecv0[side, k]
            cl = pltpu.roll(cbrecv[side * 2], lax.rem(COLS - 2 * k, COLS), 1)
            cr = pltpu.roll(cbrecv[side * 2 + 1], COLS - 2 - 2 * k, 1)
            rowfar[side * 3, k] = jnp.where(lane16 == 0, cl, pltpu.roll(h, 1, 1))
            rowfar[side * 3 + 1, k] = h
            rowfar[side * 3 + 2, k] = jnp.where(lane16 == COLS - 1, cr, pltpu.roll(h, COLS - 1, 1))
            colown[side, k] = gather(colsend0[k], own_index[side])
            for h in range(2):
                v = gather(colrecv0[side, k], far_index[side][h])
                for number, value in enumerate((pltpu.roll(v, 1, 0), v, pltpu.roll(v, ROWS - 1, 0))):
                    colfar[side * 6 + number * 2 + h, k] = value
        return carry

    lax.fori_loop(0, QUANTITIES, rows_around, 0)

    z_side = (jnp.where(gy == 0, EDGE_Z, 0.0), jnp.where(gy == n_gy - 1, EDGE_Z, 0.0))
    z_end = (jnp.where(gx == 0, EDGE_Z, 0.0), jnp.where(gx == n_gx - 1, EDGE_Z, 0.0))
    z_lane = (
        jnp.where(lane16 == 0, z_end[0], 0.0),
        jnp.zeros((SLOTS, COLS), jnp.float32),
        jnp.where(lane16 == COLS - 1, z_end[1], 0.0),
    )
    for side in range(2):
        for number in range(3):
            c = side * 3 + number
            if number != 1:
                rowfar[c, X] = rowfar[c, X] + float(number - 1)
            rowfar[c, Y] = rowfar[c, Y] + (-1.0 if side == 0 else 1.0)
            rowfar[c, Z] = rowfar[c, Z] + (z_lane[number] + z_side[side])
            for h in range(2):
                c = side * 6 + number * 2 + h
                colfar[c, X] = colfar[c, X] + (-1.0 if side == 0 else 1.0)
                z = colfar[c, Z] + z_end[side]
                if number != 1:
                    colfar[c, Y] = colfar[c, Y] + float(number - 1)
                    z = jnp.where(row == (0 if number == 0 else ROWS - 1), OUTSIDE_Z, z)
                colfar[c, Z] = z

    def scatter_rows(target, c, side, halves):
        target[c, edge_row(side), :] = target[c, edge_row(side), :] + jnp.concatenate(halves, axis=0)

    def group_sum(v):
        v = v + pltpu.roll(v, COLS - 1, 1)
        v = v + pltpu.roll(v, COLS - 2, 1)
        return v + pltpu.roll(v, COLS - 4, 1)

    ends = (lane == 0) | (lane == COLS - 1)

    def scatter_columns(target, count):
        combined = []
        for c in range(count):
            u = jnp.where((lane & 7) == 0, group_sum(coltot[0, c]), 0.0)
            combined.append(jnp.where((lane & 7) == 7, pltpu.roll(group_sum(coltot[1, c]), COLS - 1, 1), u))

        def add(p):
            for c in range(count):
                v = pltpu.roll(combined[c], lax.rem(COLS - 8 * p, COLS), 1)
                target[c, at(p), :] += jnp.where(ends, v, 0.0)

        each(SLOTS, add)

    def rim(target, count, row_mine, row_terms, col_mine, col_terms):
        def one_side(side):
            mine = row_mine(side)

            def one_row(number, totals):
                total = list(totals)
                c = side * 3 + number
                for q in range(SLOTS):
                    add = row_terms(c, q, mine)
                    for a in range(2):
                        for x, e in enumerate(add(a, ROW_AT + (c * 16 + q) * 2 + a)):
                            total[a * count + x] = total[a * count + x] + e
                return tuple(total)

            total = lax.fori_loop(0, 3, one_row, (zero,) * (2 * count))
            for x in range(count):
                scatter_rows(target, x, side, [total[x], total[count + x]])

            mine_col = col_mine(side)

            def one_column(number, totals):
                c = side * 6 + number
                return tuple(t + e for t, e in zip(totals, col_terms(c, mine_col, COL_AT + c)))

            total = lax.fori_loop(0, 6, one_column, (zero,) * count)
            for x in range(count):
                coltot[side, x] = total[x]

        each(2, one_side)
        scatter_columns(target, count)

    def first_terms(mine, other, index):
        terms = pair_terms(mine, other)
        put(index, terms)
        return terms[CO] * (other[F] - mine[F]), terms[KE]

    def first_row(c, q, mine):
        other = [rowfar[c, k, pl.ds(q, 1), :] for k in PASS1]
        return lambda a, index: first_terms(mine[a], other, index)

    rim(
        acc,
        2,
        lambda side: [[rowsend0[side, k, half(a), :] for k in PASS1] for a in range(2)],
        first_row,
        lambda side: [colown[side, k] for k in PASS1],
        lambda c, mine, index: first_terms(mine, [colfar[c, k] for k in PASS1], index),
    )
    stage_finish(1)
    stage_start(2)

    def total_of(target, per_dir, c, p):
        return target[c, at(p), :] + unshifted(*(per_dir[d, c, p] for d in range(4)))

    def set_field(p, value):
        field[at(p), :] = value
        for d, v in enumerate(shifted(value)):
            sfar[d, p] = v
        acc[0, at(p), :] = zero
        for d in range(4):
            accj[d, 0, p] = zero

    def first_update(p):
        live = p < pop[...]
        m = own[M, at(p), :]
        density = jnp.where(live, m + total_of(acc, accj, 1, p) / m, 1.0)
        inverse = 1.0 / density
        g = ROOT_HALF * inverse
        gfac[at(p), :] = g
        for d, v in enumerate(shifted(g)):
            gfar[d, p] = v
        pfac[p] = 6.0 * (HEAT_RATIO - 1.0) * inverse
        u = jnp.where(live, total_of(acc, accj, 0, p) / cap[p], 0.0)
        powers[0, p] = u
        set_field(p, u)

    each(SLOTS, first_update)

    def section_dirs(n, carry):
        d = lax.div(n, 4)
        p0 = lax.rem(n, 4) * 4
        mine = [field[at(p0 + a), :] for a in range(4)]
        ti = [zero] * 4
        for q in range(SLOTS):
            other = sfar[d, q]
            tj = None
            for a in range(4):
                t = store[CO, d * 256 + (p0 + a) * 16 + q] * (other - mine[a])
                ti[a] = ti[a] + t
                tj = t if tj is None else tj + t
            accj[d, 0, q] = accj[d, 0, q] - tj
        for a in range(4):
            acc[0, at(p0 + a), :] += ti[a]
        return carry

    def self_partners(p):
        for step in range(1, 9):
            yield lax.rem(p + step, SLOTS), SELF_AT + p * 8 + (step - 1), False
        for step in range(1, 8):
            q = lax.rem(p + SLOTS - step, SLOTS)
            yield q, SELF_AT + q * 8 + (step - 1), True

    def section_self(p):
        mine = field[at(p), :]
        ti = zero
        for q, index, _ in self_partners(p):
            ti = ti + store[CO, index] * (field[at(q), :] - mine)
        acc[0, at(p), :] += ti

    def section_row(c, q, mine):
        other = hs[FIELD, c, pl.ds(q, 1), :]
        return lambda a, index: (store[CO, index] * (other - mine[a]),)

    def drag_dirs(n, carry):
        d = lax.div(n, 8)
        p0 = lax.rem(n, 8) * 2
        g = [gfac[at(p0 + a), :] for a in range(2)]
        v = [[own[VX + c, at(p0 + a), :] for c in range(3)] for a in range(2)]
        total = [[zero] * 3 for _ in range(2)]
        for q in range(SLOTS):
            gj = gfar[d, q]
            vj = [far[d, VX + c, q] for c in range(3)]
            back = [None] * 3
            for a in range(2):
                w = store[KE, d * 256 + (p0 + a) * 16 + q] * (g[a] * gj)
                for c in range(3):
                    e = w * (vj[c] - v[a][c])
                    total[a][c] = total[a][c] + e
                    back[c] = e if back[c] is None else back[c] + e
            for c in range(3):
                kaccj[d, c, q] = kaccj[d, c, q] - back[c]
        for a in range(2):
            for c in range(3):
                kacc[c, at(p0 + a), :] += total[a][c]
        return carry

    def drag_self(p):
        g = gfac[at(p), :]
        v = [own[VX + c, at(p), :] for c in range(3)]
        total = [zero] * 3
        for q, index, _ in self_partners(p):
            w = store[KE, index] * (g * gfac[at(q), :])
            for c in range(3):
                total[c] = total[c] + w * (own[VX + c, at(q), :] - v[c])
        for c in range(3):
            kacc[c, at(p), :] += total[c]

    def drag_row(c, q, mine):
        g, v = mine
        gj = hs[DRAG, c, pl.ds(q, 1), :]
        vj = [rowfar[c, VX + x, pl.ds(q, 1), :] for x in range(3)]

        def terms(a, index):
            w = store[KE, index] * (g[a] * gj)
            return [w * (vj[x] - v[a][x]) for x in range(3)]

        return terms

    def drag_column(c, mine, index):
        g, v = mine
        w = store[KE, index] * (g * cf[DRAG, c])
        return [w * (colfar[c, VX + x] - v[x]) for x in range(3)]

    def drag_rim():
        rim(
            kacc,
            3,
            lambda side: (
                [rsend[0, side, DRAG, half(a), :] for a in range(2)],
                [[rowsend0[side, VX + x, half(a), :] for x in range(3)] for a in range(2)],
            ),
            drag_row,
            lambda side: (oc[DRAG, side], [colown[side, VX + x] for x in range(3)]),
            drag_column,
        )

    def push_dirs(n, carry):
        d = lax.div(n, 8)
        p0 = lax.rem(n, 8) * 2
        pi = [field[at(p0 + a), :] for a in range(2)]
        total = [[zero] * 3 for _ in range(2)]
        for q in range(SLOTS):
            pj = sfar[d, q]
            back = [None] * 3
            for a in range(2):
                both = pi[a] + pj
                for c in range(3):
                    e = both * store[WX + c, d * 256 + (p0 + a) * 16 + q]
                    total[a][c] = total[a][c] + e
                    back[c] = e if back[c] is None else back[c] + e
            for c in range(3):
                kaccj[d, c, q] = kaccj[d, c, q] - back[c]
        for a in range(2):
            for c in range(3):
                kacc[c, at(p0 + a), :] += total[a][c]
        return carry

    def push_self(p):
        pi = field[at(p), :]
        total = [zero] * 3
        for q, index, reverse in self_partners(p):
            both = pi + field[at(q), :]
            for c in range(3):
                e = both * store[WX + c, index]
                total[c] = total[c] - e if reverse else total[c] + e
        for c in range(3):
            kacc[c, at(p), :] += total[c]

    def push_row(c, q, mine):
        pj = hs[FIELD, c, pl.ds(q, 1), :]

        def terms(a, index):
            both = mine[a] + pj
            return [both * store[WX + x, index] for x in range(3)]

        return terms

    def push_column(c, mine, index):
        both = mine + cf[FIELD, c]
        return [both * store[WX + x, index] for x in range(3)]

    for side in range(2):
        packed = gfac[edge_row(side), :]
        for e in range(ROUNDS):
            rsend[e, side, DRAG] = packed
    packed = packed_columns(lambda p: gfac[at(p), :])
    for e in range(ROUNDS):
        vsend[e, DRAG] = packed

    polynomial = section_polynomial(SECTIONS)

    def spread(e, kind):
        for side in range(2):
            h = rrecv[e, side, kind]
            hl, hr = drecv[e, side * 2, kind], drecv[e, side * 2 + 1, kind]
            hs[kind, side * 3] = pltpu.roll(jnp.where(lane16 == COLS - 1, hl, h), 1, 1)
            hs[kind, side * 3 + 1] = h
            hs[kind, side * 3 + 2] = pltpu.roll(jnp.where(lane16 == 0, hr, h), COLS - 1, 1)
            oc[kind, side] = gather(vsend[e, kind], own_index[side])
            for h in range(2):
                v = gather(vrecv[e, side, kind], far_index[side][h])
                for number, value in enumerate((pltpu.roll(v, 1, 0), v, pltpu.roll(v, ROWS - 1, 0))):
                    cf[kind, side * 6 + number * 2 + h] = value

    def one_round(e):
        for side in range(2):
            rsend[e, side, FIELD] = field[edge_row(side), :]
        vsend[e, FIELD] = packed_columns(lambda p: field[at(p), :])
        for copy in round_copies(e):
            copy.start()

        @pl.when(e < 3)
        def _():
            lax.fori_loop(0, 16, section_dirs, 0)
            each(SLOTS, section_self)

        @pl.when(e == 0)
        def _():
            each(SLOTS, drag_self)

        @pl.when(e == 2)
        def _():
            drag_rim()

        lax.fori_loop(jnp.minimum(e * 11, 32), jnp.minimum(e * 11 + 11, 32), drag_dirs, 0)

        @pl.when(e == 3)
        def _():
            lax.fori_loop(0, 32, push_dirs, 0)
            each(SLOTS, push_self)

        for copy in round_copies(e):
            copy.wait_recv()
        each(jnp.where(e == 0, 2, 1), lambda kind: spread(e, kind))

        @pl.when(e < 3)
        def _():
            rim(
                acc,
                1,
                lambda side: [rsend[e, side, FIELD, half(a), :] for a in range(2)],
                section_row,
                lambda side: oc[FIELD, side],
                lambda c, mine, index: (store[CO, index] * (cf[FIELD, c] - mine),),
            )

        def power(p):
            return jnp.where(p < pop[...], total_of(acc, accj, 0, p) / cap[p], 0.0)

        @pl.when(e < 2)
        def _():
            def update(p):
                u = power(p)
                powers[e + 1, p] = u
                set_field(p, u)

            each(SLOTS, update)

        @pl.when(e == 2)
        def _():
            stage_finish(2)
            best = msrc[3]
            for shift in (4, 2, 1):
                best = jnp.maximum(best, pltpu.roll(best, shift, 0))
            for shift in (64, 32, 16, 8, 4, 2, 1):
                best = jnp.maximum(best, pltpu.roll(best, shift, 1))
            step_dt = COURANT / best
            msrc[4] = step_dt

            def update(p):
                y = step_dt * (polynomial[4] * power(p))
                for k in (3, 2, 1):
                    y = step_dt * (polynomial[k] * powers[k - 1, p] + y)
                y = polynomial[0] * own[F, at(p), :] + y
                heated[p] = y
                set_field(p, pfac[p] * y)

            each(SLOTS, update)

        @pl.when(e == 3)
        def _():
            rim(
                kacc,
                3,
                lambda side: [rsend[e, side, FIELD, half(a), :] for a in range(2)],
                push_row,
                lambda side: oc[FIELD, side],
                push_column,
            )

    each(ROUNDS, one_round)

    def finish(p):
        live = p < pop[...]
        scale = jnp.where(live, msrc[4] / own[M, at(p), :], 0.0)
        for c in range(3):
            moved[c, p] = own[VX + c, at(p), :] + scale * total_of(kacc, kaccj, c, p)

    each(SLOTS, finish)

    for copy in opening_copies():
        copy.wait_send()

    def sent(e):
        for copy in round_copies(e):
            copy.wait_send()

    each(ROUNDS, sent)
    for stage in range(3):
        each(stage_size[stage], lambda k, stage=stage: stage_copy(stage, k).wait_send())


def body(sizes, *args):
    f32 = jnp.float32
    messages = sum(sizes) - 3
    tile = (SLOTS, ROWS, COLS)
    vmem = pl.BlockSpec(memory_space=pltpu.VMEM)
    scratch = [pltpu.VMEM(a.shape, a.dtype) for a in args] + [
        pltpu.VMEM((QUANTITIES, FLAT, COLS), f32),
        pltpu.VMEM((4, QUANTITIES) + tile, f32),
        pltpu.VMEM((FLAT, COLS), f32),
        pltpu.VMEM((3,) + tile, f32),
        pltpu.VMEM((FLAT, COLS), f32),
        pltpu.VMEM(tile, f32),
        pltpu.VMEM((4,) + tile, f32),
        pltpu.VMEM((4,) + tile, f32),
        pltpu.VMEM((2, FLAT, COLS), f32),
        pltpu.VMEM((4, 2) + tile, f32),
        pltpu.VMEM((3, FLAT, COLS), f32),
        pltpu.VMEM((4, 3) + tile, f32),
        pltpu.VMEM((5, PAIRS, ROWS, COLS), f32),
        pltpu.VMEM((2, QUANTITIES, SLOTS, COLS), f32),
        pltpu.VMEM((2, QUANTITIES, SLOTS, COLS), f32),
        pltpu.VMEM((QUANTITIES, ROWS, COLS), f32),
        pltpu.VMEM((2, QUANTITIES, ROWS, COLS), f32),
        pltpu.VMEM((2, SLOTS, COLS), f32),
        pltpu.VMEM((4, SLOTS, COLS), f32),
        pltpu.VMEM((6, QUANTITIES, SLOTS, COLS), f32),
        pltpu.VMEM((12, QUANTITIES, ROWS, COLS), f32),
        pltpu.VMEM((2, QUANTITIES, ROWS, COLS), f32),
        pltpu.VMEM((2, 3, ROWS, COLS), f32),
        pltpu.VMEM((ROUNDS, 2, 2, SLOTS, COLS), f32),
        pltpu.VMEM((ROUNDS, 2, 2, SLOTS, COLS), f32),
        pltpu.VMEM((ROUNDS, 2, ROWS, COLS), f32),
        pltpu.VMEM((ROUNDS, 2, 2, ROWS, COLS), f32),
        pltpu.VMEM((ROUNDS, 4, 2, SLOTS, COLS), f32),
        pltpu.VMEM((2, 6, SLOTS, COLS), f32),
        pltpu.VMEM((2, 12, ROWS, COLS), f32),
        pltpu.VMEM((2, 2, ROWS, COLS), f32),
        pltpu.VMEM((5, ROWS, COLS), f32),
        pltpu.VMEM((messages, ROWS, COLS), f32),
        pltpu.SemaphoreType.DMA((ROUNDS + 1, 8)),
        pltpu.SemaphoreType.DMA((ROUNDS + 1, 8)),
        pltpu.SemaphoreType.DMA((messages,)),
        pltpu.SemaphoreType.DMA((messages,)),
        pltpu.SemaphoreType.DMA((8,)),
    ]
    return pl.pallas_call(
        functools.partial(kernel, sizes),
        out_shape=(jax.ShapeDtypeStruct(tile, f32), jax.ShapeDtypeStruct((3,) + tile, f32)),
        in_specs=[pl.BlockSpec(memory_space=pl.ANY)] * 8,
        out_specs=(vmem, vmem),
        scratch_shapes=scratch,
        compiler_params=pltpu.CompilerParams(
            collective_id=0, has_side_effects=True, vmem_limit_bytes=60 * 1024 * 1024
        ),
        name="sections_and_kick",
    )(*args)


def solution(mesh):
    n_gx, n_gy = mesh.shape["gx"], mesh.shape["gy"]
    n_hi = 4 if n_gy % 4 == 0 and n_gy > 4 else 2
    sizes = (n_gx, n_gy // n_hi, n_hi)
    cells = P("gy", "gx")
    one = P(None, "gy", "gx")
    many = P(None, None, "gy", "gx")
    return jax.shard_map(
        functools.partial(body, sizes),
        mesh=mesh,
        in_specs=(cells, many, many, one, one, one, one, many),
        out_specs=(one, many),
        check_vma=False,
    )
```

time: 67.4 us -> 66.6 us (0.988)
  local copies, waits for them, and re-layouts: 8.1 us -> 3.09 us
  Pallas kernels: 58.3 us -> 62.7 us
    unnamed x18 -> x2, local copies, waits for them, and re-layouts: 8.1 us -> 3.09 us
    pallas_call x1, Pallas kernels: 58.3 us -> 62.7 us  [body(): pl.pallas_call(functools.partial(kernel, sizes), out_shape=(jax.ShapeDtyp...]
where the time goes in v1:
time: 66.6 us; the launch traced here: 66.4 us
  Pallas kernels  62.7 us (94%)
  local copies, waits for them, and re-layouts  3.09 us (5%)
    pallas_call x1, Pallas kernels, body(): pl.pallas_call(functools.partial(kernel, sizes), out_shape=(jax.ShapeDtyp...  62.7 us
    unnamed x2, local copies, waits for them, and re-layouts  3.09 us

profile of v1, /device:TPU:1, one launch (start us, length us, event | category | flops | bytes accessed | tf_op | source)
XLA Modules:
  0.0 66.4 jit_solution(14432505239242665598)
XLA Ops:
  0.6 62.7 %sections_and_kick.1 = (f32[16,8,128]{2,1,0:T(8,128)}, f32[3,16,8,128]{3,2,1,0:T(8,128)}) custom-call(s32[8,128]{1,0:T(8,128)} %pop_in.1, f32[3,16,8,128]{3,2,1,0:T(8,128)} %loc_in.1, f32[2,16,8,128]{3,2,1,0:T(8,128)} %tilt_in.1, f32[16,8,128]{2,1,0:T(8,128)} %mass_in.1, f32[16,8,128]{2,1,0:T(8,128)} %kappa_in.1, f32[16,8,128]{2,1,0:T(8,128)} %cap_in.1, ...), custom_call_target="tpu_custom_call" | custom-call | tf_op jit(solution)/shard_map/sections_and_kick/pallas_call | solution.py:888
  63.3 1.5 %copy.12 = f32[16,8,128]{2,1,0:T(8,128)} copy(f32[16,8,128]{2,1,0:T(8,128)} %get-tuple-element.4) | data formatting | bytes 131072
  64.8 1.6 %copy.13 = f32[3,16,8,128]{3,2,1,0:T(8,128)} copy(f32[3,16,8,128]{3,2,1,0:T(8,128)} %get-tuple-element.5) | data formatting | bytes 393216

commit v2 on v1

--- a/solution.py
+++ b/solution.py
@@ -200,6 +200,14 @@
 
         lax.fori_loop(0, count, run, 0)
 
+    def grouped(count, size, fn, carry):
+        def run(k, carry):
+            for a in range(size):
+                carry = fn(k * size + a, carry)
+            return carry
+
+        return lax.fori_loop(0, count // size, run, carry)
+
     barrier = pltpu.get_barrier_semaphore()
 
     def greet(device):
@@ -278,7 +286,7 @@
 
     for load in loads:
         load.wait()
-    msrc[0] = lax.fori_loop(0, SLOTS, prepare, zero)
+    msrc[0] = grouped(SLOTS, 4, prepare, zero)
 
     def pack(k, cb):
         cb = list(cb)
@@ -291,7 +299,7 @@
         return tuple(cb)
 
     blank = jnp.zeros((SLOTS, COLS), jnp.float32)
-    cbsend[0], cbsend[1] = lax.fori_loop(0, QUANTITIES, pack, (blank, blank))
+    cbsend[0], cbsend[1] = grouped(QUANTITIES, 3, pack, (blank, blank))
 
     def remote(src, dst, s, r, device):
         return pltpu.make_async_remote_copy(
@@ -440,7 +448,7 @@
                     colfar[side * 6 + number * 2 + h, k] = value
         return carry
 
-    lax.fori_loop(0, QUANTITIES, rows_around, 0)
+    grouped(QUANTITIES, 4, rows_around, 0)
 
     z_side = (jnp.where(gy == 0, EDGE_Z, 0.0), jnp.where(gy == n_gy - 1, EDGE_Z, 0.0))
     z_end = (jnp.where(gx == 0, EDGE_Z, 0.0), jnp.where(gx == n_gx - 1, EDGE_Z, 0.0))
@@ -483,10 +491,11 @@
 
         def add(p):
             for c in range(count):
-                v = pltpu.roll(combined[c], lax.rem(COLS - 8 * p, COLS), 1)
+                v = pltpu.roll(combined[c], (COLS - 8 * p) % COLS, 1) if p else combined[c]
                 target[c, at(p), :] += jnp.where(ends, v, 0.0)
 
-        each(SLOTS, add)
+        for p in range(SLOTS):
+            add(p)
 
     def rim(target, count, row_mine, row_terms, col_mine, col_terms):
         def one_side(side):
@@ -502,7 +511,12 @@
                             total[a * count + x] = total[a * count + x] + e
                 return tuple(total)
 
-            total = lax.fori_loop(0, 3, one_row, (zero,) * (2 * count))
+            total = (zero,) * (2 * count)
+            if count == 1:
+                for number in range(3):
+                    total = one_row(number, total)
+            else:
+                total = lax.fori_loop(0, 3, one_row, total)
             for x in range(count):
                 scatter_rows(target, x, side, [total[x], total[count + x]])
 
@@ -512,11 +526,14 @@
                 c = side * 6 + number
                 return tuple(t + e for t, e in zip(totals, col_terms(c, mine_col, COL_AT + c)))
 
-            total = lax.fori_loop(0, 6, one_column, (zero,) * count)
+            total = (zero,) * count
+            for number in range(6):
+                total = one_column(number, total)
             for x in range(count):
                 coltot[side, x] = total[x]
 
-        each(2, one_side)
+        for side in range(2):
+            one_side(side)
         scatter_columns(target, count)
 
     def first_terms(mine, other, index):
@@ -564,7 +581,8 @@
         powers[0, p] = u
         set_field(p, u)
 
-    each(SLOTS, first_update)
+    for p in range(SLOTS):
+        first_update(p)
 
     def section_dirs(n, carry):
         d = lax.div(n, 4)
@@ -739,32 +757,28 @@
         for copy in round_copies(e):
             copy.start()
 
-        @pl.when(e < 3)
-        def _():
+        if e < 3:
             lax.fori_loop(0, 16, section_dirs, 0)
             each(SLOTS, section_self)
 
-        @pl.when(e == 0)
-        def _():
+        if e == 0:
             each(SLOTS, drag_self)
 
-        @pl.when(e == 2)
-        def _():
+        if e == 2:
             drag_rim()
 
-        lax.fori_loop(jnp.minimum(e * 11, 32), jnp.minimum(e * 11 + 11, 32), drag_dirs, 0)
-
-        @pl.when(e == 3)
-        def _():
+        lax.fori_loop(min(e * 11, 32), min(e * 11 + 11, 32), drag_dirs, 0)
+
+        if e == 3:
             lax.fori_loop(0, 32, push_dirs, 0)
             each(SLOTS, push_self)
 
         for copy in round_copies(e):
             copy.wait_recv()
-        each(jnp.where(e == 0, 2, 1), lambda kind: spread(e, kind))
-
-        @pl.when(e < 3)
-        def _():
+        for kind in range(2 if e == 0 else 1):
+            spread(e, kind)
+
+        if e < 3:
             rim(
                 acc,
                 1,
@@ -777,25 +791,27 @@
         def power(p):
             return jnp.where(p < pop[...], total_of(acc, accj, 0, p) / cap[p], 0.0)
 
-        @pl.when(e < 2)
-        def _():
-            def update(p):
-                u = power(p)
-                powers[e + 1, p] = u
-                set_field(p, u)
-
-            each(SLOTS, update)
-
-        @pl.when(e == 2)
-        def _():
+        if e == 1:
             stage_finish(2)
             best = msrc[3]
             for shift in (4, 2, 1):
                 best = jnp.maximum(best, pltpu.roll(best, shift, 0))
             for shift in (64, 32, 16, 8, 4, 2, 1):
                 best = jnp.maximum(best, pltpu.roll(best, shift, 1))
-            step_dt = COURANT / best
-            msrc[4] = step_dt
+            msrc[4] = COURANT / best
+
+        if e < 2:
+
+            def update(p):
+                u = power(p)
+                powers[e + 1, p] = u
+                set_field(p, u)
+
+            for p in range(SLOTS):
+                update(p)
+
+        if e == 2:
+            step_dt = msrc[4]
 
             def update(p):
                 y = step_dt * (polynomial[4] * power(p))
@@ -805,10 +821,10 @@
                 heated[p] = y
                 set_field(p, pfac[p] * y)
 
-            each(SLOTS, update)
-
-        @pl.when(e == 3)
-        def _():
+            for p in range(SLOTS):
+                update(p)
+
+        if e == 3:
             rim(
                 kacc,
                 3,
@@ -818,7 +834,8 @@
                 push_column,
             )
 
-    each(ROUNDS, one_round)
+    for e in range(ROUNDS):
+        one_round(e)
 
     def finish(p):
         live = p < pop[...]
@@ -826,7 +843,8 @@
         for c in range(3):
             moved[c, p] = own[VX + c, at(p), :] + scale * total_of(kacc, kaccj, c, p)
 
-    each(SLOTS, finish)
+    for p in range(SLOTS):
+        finish(p)
 
     for copy in opening_copies():
         copy.wait_send()

time: 66.6 us -> 51.2 us (0.77)
  Pallas kernels: 62.7 us -> 47.3 us
    pallas_call x1, Pallas kernels: 62.7 us -> 47.3 us  [body(): pl.pallas_call(functools.partial(kernel, sizes), out_shape=(jax.ShapeDtyp...]
where the time goes in v2:
time: 51.2 us; the launch traced here: 51.1 us
  Pallas kernels  47.3 us (92%)
  local copies, waits for them, and re-layouts  3.09 us (6%)
  between operations  0.64 us (1%)
    pallas_call x1, Pallas kernels, body(): pl.pallas_call(functools.partial(kernel, sizes), out_shape=(jax.ShapeDtyp...  47.3 us
    unnamed x2, local copies, waits for them, and re-layouts  3.09 us

profile of v2, /device:TPU:1, one launch (start us, length us, event | category | flops | bytes accessed | tf_op | source)
XLA Modules:
  0.0 51.1 jit_solution(10385738311074798151)
XLA Ops:
  0.6 47.3 %sections_and_kick.1 = (f32[16,8,128]{2,1,0:T(8,128)}, f32[3,16,8,128]{3,2,1,0:T(8,128)}) custom-call(s32[8,128]{1,0:T(8,128)} %pop_in.1, f32[3,16,8,128]{3,2,1,0:T(8,128)} %loc_in.1, f32[2,16,8,128]{3,2,1,0:T(8,128)} %tilt_in.1, f32[16,8,128]{2,1,0:T(8,128)} %mass_in.1, f32[16,8,128]{2,1,0:T(8,128)} %kappa_in.1, f32[16,8,128]{2,1,0:T(8,128)} %cap_in.1, ...), custom_call_target="tpu_custom_call" | custom-call | tf_op jit(solution)/shard_map/sections_and_kick/pallas_call | solution.py:906
  48.0 1.5 %copy.12 = f32[16,8,128]{2,1,0:T(8,128)} copy(f32[16,8,128]{2,1,0:T(8,128)} %get-tuple-element.4) | data formatting | bytes 131072
  49.4 1.6 %copy.13 = f32[3,16,8,128]{3,2,1,0:T(8,128)} copy(f32[3,16,8,128]{3,2,1,0:T(8,128)} %get-tuple-element.5) | data formatting | bytes 393216

commit v3 on v2

--- a/solution.py
+++ b/solution.py
@@ -22,10 +22,10 @@
 X, Y, Z, BX, BY, BZ, KA, F, M, VX, VY, VZ = range(12)
 QUANTITIES = 12
 
-DIRS = ((0, 1), (1, -1), (1, 0), (1, 1))
+DIRECTIONS = 4
 
 CO, KE, WX, WY, WZ = range(5)
-SELF_AT = len(DIRS) * SLOTS * SLOTS
+SELF_AT = DIRECTIONS * SLOTS * SLOTS
 ROW_AT = SELF_AT + SLOTS * 8
 COL_AT = ROW_AT + 6 * SLOTS * 2
 PAIRS = COL_AT + 12
@@ -34,8 +34,9 @@
 FIELD, DRAG = range(2)
 
 EMPTY_Z = 10.0
-OUTSIDE_Z = 20.0
+OUTSIDE_X = 20.0
 EDGE_Z = 40.0
+PAD = 8
 
 SIN = (0.9999999957157406, -0.1666665796974384, 0.008333050613415454, -0.0001980904606136566, 2.605165590448684e-06)
 COS = (
@@ -116,11 +117,8 @@
     cap,
     temp,
     mot,
-    own,
     far,
-    field,
     powers,
-    gfac,
     pfac,
     sfar,
     gfar,
@@ -155,6 +153,7 @@
     mrecv_sem,
     load_sem,
 ):
+    own, field, gfac = far.at[2], sfar.at[2], gfar.at[2]
     loads = [
         pltpu.make_async_copy(src, dst, load_sem.at[number])
         for number, (src, dst) in enumerate(
@@ -208,6 +207,19 @@
 
         return lax.fori_loop(0, count // size, run, carry)
 
+    def over(fn, first, last, split):
+        if first < split:
+            lax.fori_loop(first, split, functools.partial(fn, 0), 0)
+        if last > split:
+            lax.fori_loop(max(first, split), last, functools.partial(fn, 1), 0)
+
+    def paired(fn):
+        def both(p):
+            fn(2 * p)
+            fn(2 * p + 1)
+
+        each(SLOTS // 2, both)
+
     barrier = pltpu.get_barrier_semaphore()
 
     def greet(device):
@@ -222,6 +234,7 @@
     row = lax.broadcasted_iota(jnp.int32, (ROWS, COLS), 0)
     lane16 = lax.broadcasted_iota(jnp.int32, (SLOTS, COLS), 1)
     zero = jnp.zeros((ROWS, COLS), jnp.float32)
+    rows_down = row.astype(jnp.float32)
 
     def at(p):
         start = p * ROWS
@@ -233,12 +246,17 @@
     def half(a):
         return pl.ds(a * 8, 8)
 
-    def shifted(v):
-        low = pltpu.roll(v, ROWS - 1, 0)
-        return (pltpu.roll(v, COLS - 1, 1), pltpu.roll(low, 1, 1), low, pltpu.roll(low, COLS - 1, 1))
-
-    def unshifted(a, b, c, d):
-        return pltpu.roll(a, 1, 1) + pltpu.roll(pltpu.roll(b, COLS - 1, 1) + c + pltpu.roll(d, 1, 1), 1, 0)
+    def partner(q, off):
+        return pl.ds(q * ROWS + off, ROWS)
+
+    def slot_sum(q):
+        start = PAD + q * ROWS
+        return pl.ds(start if isinstance(q, int) else pl.multiple_of(start, ROWS), ROWS)
+
+    def put_copies(target, k, p, value):
+        target[(0, *k, at(p))] = pltpu.roll(value, COLS - 1, 1)
+        target[(1, *k, at(p))] = pltpu.roll(value, 1, 1)
+        target[(2, *k, at(p))] = value
 
     def gather(v, index):
         return jnp.take_along_axis(v, index, axis=1)
@@ -266,7 +284,7 @@
         v = [mot[c, p] for c in range(3)]
         values = [
             loc[0, p],
-            loc[1, p],
+            loc[1, p] + rows_down,
             jnp.where(live, loc[2, p], EMPTY_Z),
             ROOT_HALF * (sin_p * cos_a),
             ROOT_HALF * (sin_p * sin_a),
@@ -284,6 +302,17 @@
         speed = jnp.sqrt(HEAT_RATIO * (HEAT_RATIO - 1.0) * t) + jnp.sqrt(v[0] * v[0] + v[1] * v[1] + v[2] * v[2])
         return jnp.maximum(fastest, jnp.where(live, speed, 0.0))
 
+    after = pl.ds(FLAT, PAD)
+    for copy in range(3):
+        for k in range(QUANTITIES):
+            far[copy, k, after, :] = zero
+        sfar[copy, after, :] = zero
+        gfar[copy, after, :] = zero
+    for d in range(DIRECTIONS):
+        for c in range(2):
+            accj[d, c, pl.ds(0, PAD), :] = zero
+        for c in range(3):
+            kaccj[d, c, pl.ds(0, PAD), :] = zero
     for load in loads:
         load.wait()
     msrc[0] = grouped(SLOTS, 4, prepare, zero)
@@ -334,7 +363,7 @@
             (cbsend.at[1], cbrecv.at[0]),
         )
         return [
-            remote(src, dst, send_sem.at[ROUNDS, c], recv_sem.at[ROUNDS, c], around[c])
+            remote(src, dst, send_sem.at[c], recv_sem.at[1, c], around[c])
             for c, (src, dst) in enumerate(plan)
         ]
 
@@ -350,7 +379,7 @@
             (rsend.at[e, 1], drecv.at[e, 0]),
         )
         return [
-            remote(src, dst, send_sem.at[e, c], recv_sem.at[e, c], around[c]) for c, (src, dst) in enumerate(plan)
+            remote(src, dst, send_sem.at[c], recv_sem.at[e % 2, c], around[c]) for c, (src, dst) in enumerate(plan)
         ]
 
     pl.semaphore_wait(barrier, len(around) + sum(stage_size))
@@ -376,39 +405,33 @@
             ti = ti + t
             ri = ri + terms[KE]
             if step < 8:
-                acc[0, at(q), :] += -t
+                acc[0, at(q), :] -= t
                 acc[1, at(q), :] += terms[KE]
         acc[0, at(p), :] += ti
         acc[1, at(p), :] += ri
         for k in range(QUANTITIES):
-            for d, v in enumerate(shifted(own[k, at(p), :])):
-                if k == X and DIRS[d][1]:
-                    v = v + float(DIRS[d][1])
-                if k == Y and DIRS[d][0]:
-                    v = v + float(DIRS[d][0])
-                if k == Z:
-                    out = None
-                    for step, index, last in ((DIRS[d][0], row, ROWS - 1), (DIRS[d][1], lane, COLS - 1)):
-                        if step:
-                            hit = index == (last if step > 0 else 0)
-                            out = hit if out is None else out | hit
-                    v = jnp.where(out, OUTSIDE_Z, v)
-                far[d, k, p] = v
-        for d in range(4):
+            value = own[k, at(p), :]
+            east, west = pltpu.roll(value, COLS - 1, 1), pltpu.roll(value, 1, 1)
+            if k == X:
+                east = jnp.where(lane == COLS - 1, OUTSIDE_X, east + 1.0)
+                west = jnp.where(lane == 0, OUTSIDE_X, west - 1.0)
+            far[0, k, at(p), :] = east
+            far[1, k, at(p), :] = west
+        for d in range(DIRECTIONS):
             for c in range(2):
-                accj[d, c, p] = zero
+                accj[d, c, slot_sum(p), :] = zero
             for c in range(3):
-                kaccj[d, c, p] = zero
+                kaccj[d, c, slot_sum(p), :] = zero
         return carry
 
-    def first_dirs(n, carry):
+    def first_dirs(off, n, carry):
         d = lax.div(n, 8)
         p0 = lax.rem(n, 8) * 2
         mine = [[own[k, at(p0 + a), :] for k in PASS1] for a in range(2)]
         ti = [zero, zero]
         ri = [zero, zero]
         for q in range(SLOTS):
-            other = [far[d, k, q] for k in PASS1]
+            other = [far[lax.rem(d, 3), k, partner(q, off), :] for k in PASS1]
             tj, rj = None, None
             for a in range(2):
                 terms = pair_terms(mine[a], other)
@@ -418,15 +441,15 @@
                 ri[a] = ri[a] + r
                 tj = t if tj is None else tj + t
                 rj = r if rj is None else rj + r
-            accj[d, 0, q] = accj[d, 0, q] - tj
-            accj[d, 1, q] = accj[d, 1, q] + rj
+            accj[d, 0, slot_sum(q), :] -= tj
+            accj[d, 1, slot_sum(q), :] += rj
         for a in range(2):
             acc[0, at(p0 + a), :] += ti[a]
             acc[1, at(p0 + a), :] += ri[a]
         return carry
 
     lax.fori_loop(0, SLOTS, first_self, 0)
-    lax.fori_loop(0, 32, first_dirs, 0)
+    over(first_dirs, 0, 32, 8)
     stage_finish(0)
     stage_start(1)
 
@@ -462,16 +485,12 @@
             c = side * 3 + number
             if number != 1:
                 rowfar[c, X] = rowfar[c, X] + float(number - 1)
-            rowfar[c, Y] = rowfar[c, Y] + (-1.0 if side == 0 else 1.0)
+            rowfar[c, Y] = rowfar[c, Y] + float(-ROWS if side == 0 else ROWS)
             rowfar[c, Z] = rowfar[c, Z] + (z_lane[number] + z_side[side])
             for h in range(2):
                 c = side * 6 + number * 2 + h
                 colfar[c, X] = colfar[c, X] + (-1.0 if side == 0 else 1.0)
-                z = colfar[c, Z] + z_end[side]
-                if number != 1:
-                    colfar[c, Y] = colfar[c, Y] + float(number - 1)
-                    z = jnp.where(row == (0 if number == 0 else ROWS - 1), OUTSIDE_Z, z)
-                colfar[c, Z] = z
+                colfar[c, Z] = colfar[c, Z] + z_end[side]
 
     def scatter_rows(target, c, side, halves):
         target[c, edge_row(side), :] = target[c, edge_row(side), :] + jnp.concatenate(halves, axis=0)
@@ -557,15 +576,19 @@
     stage_start(2)
 
     def total_of(target, per_dir, c, p):
-        return target[c, at(p), :] + unshifted(*(per_dir[d, c, p] for d in range(4)))
+        below = pl.ds(PAD + p * ROWS - 1, ROWS)
+        east = per_dir[0, c, slot_sum(p), :] + per_dir[3, c, below, :]
+        west = per_dir[1, c, below, :]
+        total = target[c, at(p), :] + per_dir[2, c, below, :]
+        return total + pltpu.roll(east, 1, 1) + pltpu.roll(west, COLS - 1, 1)
+
+    def clear(p):
+        acc[0, at(p), :] = zero
+        for d in range(DIRECTIONS):
+            accj[d, 0, slot_sum(p), :] = zero
 
     def set_field(p, value):
-        field[at(p), :] = value
-        for d, v in enumerate(shifted(value)):
-            sfar[d, p] = v
-        acc[0, at(p), :] = zero
-        for d in range(4):
-            accj[d, 0, p] = zero
+        put_copies(sfar, (), p, value)
 
     def first_update(p):
         live = p < pop[...]
@@ -573,9 +596,7 @@
         density = jnp.where(live, m + total_of(acc, accj, 1, p) / m, 1.0)
         inverse = 1.0 / density
         g = ROOT_HALF * inverse
-        gfac[at(p), :] = g
-        for d, v in enumerate(shifted(g)):
-            gfar[d, p] = v
+        put_copies(gfar, (), p, g)
         pfac[p] = 6.0 * (HEAT_RATIO - 1.0) * inverse
         u = jnp.where(live, total_of(acc, accj, 0, p) / cap[p], 0.0)
         powers[0, p] = u
@@ -583,29 +604,34 @@
 
     for p in range(SLOTS):
         first_update(p)
-
-    def section_dirs(n, carry):
+    for p in range(SLOTS):
+        clear(p)
+
+    def section_dirs(off, n, carry):
         d = lax.div(n, 4)
         p0 = lax.rem(n, 4) * 4
         mine = [field[at(p0 + a), :] for a in range(4)]
         ti = [zero] * 4
         for q in range(SLOTS):
-            other = sfar[d, q]
+            other = sfar[lax.rem(d, 3), partner(q, off), :]
             tj = None
             for a in range(4):
                 t = store[CO, d * 256 + (p0 + a) * 16 + q] * (other - mine[a])
                 ti[a] = ti[a] + t
                 tj = t if tj is None else tj + t
-            accj[d, 0, q] = accj[d, 0, q] - tj
+            accj[d, 0, slot_sum(q), :] -= tj
         for a in range(4):
             acc[0, at(p0 + a), :] += ti[a]
         return carry
 
+    def wrap(p):
+        return p % SLOTS if isinstance(p, int) else lax.rem(p, SLOTS)
+
     def self_partners(p):
         for step in range(1, 9):
-            yield lax.rem(p + step, SLOTS), SELF_AT + p * 8 + (step - 1), False
+            yield wrap(p + step), SELF_AT + p * 8 + (step - 1), False
         for step in range(1, 8):
-            q = lax.rem(p + SLOTS - step, SLOTS)
+            q = wrap(p + SLOTS - step)
             yield q, SELF_AT + q * 8 + (step - 1), True
 
     def section_self(p):
@@ -619,15 +645,15 @@
         other = hs[FIELD, c, pl.ds(q, 1), :]
         return lambda a, index: (store[CO, index] * (other - mine[a]),)
 
-    def drag_dirs(n, carry):
+    def drag_dirs(off, n, carry):
         d = lax.div(n, 8)
         p0 = lax.rem(n, 8) * 2
         g = [gfac[at(p0 + a), :] for a in range(2)]
         v = [[own[VX + c, at(p0 + a), :] for c in range(3)] for a in range(2)]
         total = [[zero] * 3 for _ in range(2)]
         for q in range(SLOTS):
-            gj = gfar[d, q]
-            vj = [far[d, VX + c, q] for c in range(3)]
+            gj = gfar[lax.rem(d, 3), partner(q, off), :]
+            vj = [far[lax.rem(d, 3), VX + c, partner(q, off), :] for c in range(3)]
             back = [None] * 3
             for a in range(2):
                 w = store[KE, d * 256 + (p0 + a) * 16 + q] * (g[a] * gj)
@@ -636,7 +662,7 @@
                     total[a][c] = total[a][c] + e
                     back[c] = e if back[c] is None else back[c] + e
             for c in range(3):
-                kaccj[d, c, q] = kaccj[d, c, q] - back[c]
+                kaccj[d, c, slot_sum(q), :] -= back[c]
         for a in range(2):
             for c in range(3):
                 kacc[c, at(p0 + a), :] += total[a][c]
@@ -682,13 +708,13 @@
             drag_column,
         )
 
-    def push_dirs(n, carry):
+    def push_dirs(off, n, carry):
         d = lax.div(n, 8)
         p0 = lax.rem(n, 8) * 2
         pi = [field[at(p0 + a), :] for a in range(2)]
         total = [[zero] * 3 for _ in range(2)]
         for q in range(SLOTS):
-            pj = sfar[d, q]
+            pj = sfar[lax.rem(d, 3), partner(q, off), :]
             back = [None] * 3
             for a in range(2):
                 both = pi[a] + pj
@@ -697,7 +723,7 @@
                     total[a][c] = total[a][c] + e
                     back[c] = e if back[c] is None else back[c] + e
             for c in range(3):
-                kaccj[d, c, q] = kaccj[d, c, q] - back[c]
+                kaccj[d, c, slot_sum(q), :] -= back[c]
         for a in range(2):
             for c in range(3):
                 kacc[c, at(p0 + a), :] += total[a][c]
@@ -754,24 +780,29 @@
         for side in range(2):
             rsend[e, side, FIELD] = field[edge_row(side), :]
         vsend[e, FIELD] = packed_columns(lambda p: field[at(p), :])
+        for copy in round_copies(e - 1) if e else opening_copies():
+            copy.wait_send()
         for copy in round_copies(e):
             copy.start()
 
         if e < 3:
-            lax.fori_loop(0, 16, section_dirs, 0)
-            each(SLOTS, section_self)
+            over(section_dirs, 0, 16, 4)
+            for p in range(SLOTS):
+                section_self(p)
 
         if e == 0:
-            each(SLOTS, drag_self)
+            paired(drag_self)
 
         if e == 2:
             drag_rim()
 
-        lax.fori_loop(min(e * 11, 32), min(e * 11 + 11, 32), drag_dirs, 0)
+        if e < 3:
+            over(drag_dirs, (0, 8, 20)[e], (8, 20, 32)[e], 8)
 
         if e == 3:
-            lax.fori_loop(0, 32, push_dirs, 0)
-            each(SLOTS, push_self)
+            over(push_dirs, 0, 32, 8)
+            for p in range(SLOTS):
+                push_self(p)
 
         for copy in round_copies(e):
             copy.wait_recv()
@@ -809,6 +840,8 @@
 
             for p in range(SLOTS):
                 update(p)
+            for p in range(SLOTS):
+                clear(p)
 
         if e == 2:
             step_dt = msrc[4]
@@ -846,16 +879,21 @@
     for p in range(SLOTS):
         finish(p)
 
-    for copy in opening_copies():
+    for copy in round_copies(ROUNDS - 1):
         copy.wait_send()
-
-    def sent(e):
-        for copy in round_copies(e):
-            copy.wait_send()
-
-    each(ROUNDS, sent)
     for stage in range(3):
         each(stage_size[stage], lambda k, stage=stage: stage_copy(stage, k).wait_send())
+
+
+def hand_over(heated_in, moved_in, heated, moved, sem):
+    copies = [
+        pltpu.make_async_copy(heated_in, heated, sem.at[0]),
+        pltpu.make_async_copy(moved_in, moved, sem.at[1]),
+    ]
+    for copy in copies:
+        copy.start()
+    for copy in copies:
+        copy.wait()
 
 
 def body(sizes, *args):
@@ -864,18 +902,15 @@
     tile = (SLOTS, ROWS, COLS)
     vmem = pl.BlockSpec(memory_space=pltpu.VMEM)
     scratch = [pltpu.VMEM(a.shape, a.dtype) for a in args] + [
-        pltpu.VMEM((QUANTITIES, FLAT, COLS), f32),
-        pltpu.VMEM((4, QUANTITIES) + tile, f32),
-        pltpu.VMEM((FLAT, COLS), f32),
+        pltpu.VMEM((3, QUANTITIES, FLAT + PAD, COLS), f32),
         pltpu.VMEM((3,) + tile, f32),
-        pltpu.VMEM((FLAT, COLS), f32),
         pltpu.VMEM(tile, f32),
-        pltpu.VMEM((4,) + tile, f32),
-        pltpu.VMEM((4,) + tile, f32),
+        pltpu.VMEM((3, FLAT + PAD, COLS), f32),
+        pltpu.VMEM((3, FLAT + PAD, COLS), f32),
         pltpu.VMEM((2, FLAT, COLS), f32),
-        pltpu.VMEM((4, 2) + tile, f32),
+        pltpu.VMEM((DIRECTIONS, 2, PAD + FLAT, COLS), f32),
         pltpu.VMEM((3, FLAT, COLS), f32),
-        pltpu.VMEM((4, 3) + tile, f32),
+        pltpu.VMEM((DIRECTIONS, 3, PAD + FLAT, COLS), f32),
         pltpu.VMEM((5, PAIRS, ROWS, COLS), f32),
         pltpu.VMEM((2, QUANTITIES, SLOTS, COLS), f32),
         pltpu.VMEM((2, QUANTITIES, SLOTS, COLS), f32),
@@ -897,15 +932,16 @@
         pltpu.VMEM((2, 2, ROWS, COLS), f32),
         pltpu.VMEM((5, ROWS, COLS), f32),
         pltpu.VMEM((messages, ROWS, COLS), f32),
-        pltpu.SemaphoreType.DMA((ROUNDS + 1, 8)),
-        pltpu.SemaphoreType.DMA((ROUNDS + 1, 8)),
+        pltpu.SemaphoreType.DMA((8,)),
+        pltpu.SemaphoreType.DMA((2, 8)),
         pltpu.SemaphoreType.DMA((messages,)),
         pltpu.SemaphoreType.DMA((messages,)),
         pltpu.SemaphoreType.DMA((8,)),
     ]
-    return pl.pallas_call(
+    shapes = (jax.ShapeDtypeStruct(tile, f32), jax.ShapeDtypeStruct((3,) + tile, f32))
+    results = pl.pallas_call(
         functools.partial(kernel, sizes),
-        out_shape=(jax.ShapeDtypeStruct(tile, f32), jax.ShapeDtypeStruct((3,) + tile, f32)),
+        out_shape=shapes,
         in_specs=[pl.BlockSpec(memory_space=pl.ANY)] * 8,
         out_specs=(vmem, vmem),
         scratch_shapes=scratch,
@@ -914,6 +950,16 @@
         ),
         name="sections_and_kick",
     )(*args)
+    anywhere = pl.BlockSpec(memory_space=pl.ANY)
+    return pl.pallas_call(
+        hand_over,
+        out_shape=shapes,
+        in_specs=[anywhere] * 2,
+        out_specs=(anywhere, anywhere),
+        scratch_shapes=[pltpu.SemaphoreType.DMA((2,))],
+        compiler_params=pltpu.CompilerParams(vmem_limit_bytes=60 * 1024 * 1024),
+        name="hand_over",
+    )(*results)
 
 
 def solution(mesh):

time: 51.2 us -> 55.4 us (1.082)
  Pallas kernels: 47.3 us -> 54.6 us
  local copies, waits for them, and re-layouts: 3.09 us -> 0 us
    pallas_call x1 -> x2, Pallas kernels: 47.3 us -> 54.6 us  [the longest x1 45.6 us: body(): pl.pallas_call(functools.partial(kernel, sizes), out_shape=shapes, in_spe...]
    unnamed x2 -> x0, local copies, waits for them, and re-layouts: 3.09 us -> none
where the time goes in v3:
time: 55.4 us; the launch traced here: 55.3 us
  Pallas kernels  54.6 us (99%)
  between operations  0.64 us (1%)
    pallas_call x1, Pallas kernels, body(): pl.pallas_call(functools.partial(kernel, sizes), out_shape=shapes, in_spe...  45.6 us
    pallas_call x1, Pallas kernels, body(): pl.pallas_call(hand_over, out_shape=shapes, in_specs=[anywhere] * 2, out_...  9.06 us

profile of v3, /device:TPU:1, one launch (start us, length us, event | category | flops | bytes accessed | tf_op | source)
XLA Modules:
  0.0 55.3 jit_solution(10134503011148777190)
XLA Ops:
  0.6 45.6 %sections_and_kick.1 = (f32[16,8,128]{2,1,0:T(8,128)}, f32[3,16,8,128]{3,2,1,0:T(8,128)}) custom-call(s32[8,128]{1,0:T(8,128)} %pop_in.1, f32[3,16,8,128]{3,2,1,0:T(8,128)} %loc_in.1, f32[2,16,8,128]{3,2,1,0:T(8,128)} %tilt_in.1, f32[16,8,128]{2,1,0:T(8,128)} %mass_in.1, f32[16,8,128]{2,1,0:T(8,128)} %kappa_in.1, f32[16,8,128]{2,1,0:T(8,128)} %cap_in.1, ...), custom_call_target="tpu_custom_call" | custom-call | tf_op jit(solution)/shard_map/sections_and_kick/pallas_call | solution.py:942
  46.2 9.1 %hand_over.1 = (f32[16,8,128]{2,1,0:T(8,128)}, f32[3,16,8,128]{3,2,1,0:T(8,128)}) custom-call(f32[16,8,128]{2,1,0:T(8,128)} %get-tuple-element.4.heated_in, f32[3,16,8,128]{3,2,1,0:T(8,128)} %get-tuple-element.5.moved_in), custom_call_target="tpu_custom_call" | custom-call | tf_op jit(solution)/shard_map/hand_over/pallas_call | solution.py:954

commit v4 on v3

--- a/solution.py
+++ b/solution.py
@@ -368,15 +368,16 @@
         ]
 
     def round_copies(e):
+        kinds = pl.ds(0, 2 if e == 0 else 1)
         plan = (
-            (rsend.at[e, 0], rrecv.at[e, 1]),
-            (rsend.at[e, 1], rrecv.at[e, 0]),
-            (vsend.at[e], vrecv.at[e, 1]),
-            (vsend.at[e], vrecv.at[e, 0]),
-            (rsend.at[e, 0], drecv.at[e, 3]),
-            (rsend.at[e, 0], drecv.at[e, 2]),
-            (rsend.at[e, 1], drecv.at[e, 1]),
-            (rsend.at[e, 1], drecv.at[e, 0]),
+            (rsend.at[e, 0, kinds], rrecv.at[e, 1, kinds]),
+            (rsend.at[e, 1, kinds], rrecv.at[e, 0, kinds]),
+            (vsend.at[e, kinds], vrecv.at[e, 1, kinds]),
+            (vsend.at[e, kinds], vrecv.at[e, 0, kinds]),
+            (rsend.at[e, 0, kinds], drecv.at[e, 3, kinds]),
+            (rsend.at[e, 0, kinds], drecv.at[e, 2, kinds]),
+            (rsend.at[e, 1, kinds], drecv.at[e, 1, kinds]),
+            (rsend.at[e, 1, kinds], drecv.at[e, 0, kinds]),
         )
         return [
             remote(src, dst, send_sem.at[c], recv_sem.at[e % 2, c], around[c]) for c, (src, dst) in enumerate(plan)
@@ -572,9 +573,6 @@
         lambda side: [colown[side, k] for k in PASS1],
         lambda c, mine, index: first_terms(mine, [colfar[c, k] for k in PASS1], index),
     )
-    stage_finish(1)
-    stage_start(2)
-
     def total_of(target, per_dir, c, p):
         below = pl.ds(PAD + p * ROWS - 1, ROWS)
         east = per_dir[0, c, slot_sum(p), :] + per_dir[3, c, below, :]
@@ -755,11 +753,9 @@
 
     for side in range(2):
         packed = gfac[edge_row(side), :]
-        for e in range(ROUNDS):
-            rsend[e, side, DRAG] = packed
+        rsend[0, side, DRAG] = packed
     packed = packed_columns(lambda p: gfac[at(p), :])
-    for e in range(ROUNDS):
-        vsend[e, DRAG] = packed
+    vsend[0, DRAG] = packed
 
     polynomial = section_polynomial(SECTIONS)
 
@@ -804,6 +800,18 @@
             for p in range(SLOTS):
                 push_self(p)
 
+        if e == 0:
+            stage_finish(1)
+            stage_start(2)
+        if e == 2:
+            stage_finish(2)
+            best = msrc[3]
+            for shift in (4, 2, 1):
+                best = jnp.maximum(best, pltpu.roll(best, shift, 0))
+            for shift in (64, 32, 16, 8, 4, 2, 1):
+                best = jnp.maximum(best, pltpu.roll(best, shift, 1))
+            msrc[4] = COURANT / best
+
         for copy in round_copies(e):
             copy.wait_recv()
         for kind in range(2 if e == 0 else 1):
@@ -822,15 +830,6 @@
         def power(p):
             return jnp.where(p < pop[...], total_of(acc, accj, 0, p) / cap[p], 0.0)
 
-        if e == 1:
-            stage_finish(2)
-            best = msrc[3]
-            for shift in (4, 2, 1):
-                best = jnp.maximum(best, pltpu.roll(best, shift, 0))
-            for shift in (64, 32, 16, 8, 4, 2, 1):
-                best = jnp.maximum(best, pltpu.roll(best, shift, 1))
-            msrc[4] = COURANT / best
-
         if e < 2:
 
             def update(p):
@@ -885,15 +884,17 @@
         each(stage_size[stage], lambda k, stage=stage: stage_copy(stage, k).wait_send())
 
 
-def hand_over(heated_in, moved_in, heated, moved, sem):
-    copies = [
-        pltpu.make_async_copy(heated_in, heated, sem.at[0]),
-        pltpu.make_async_copy(moved_in, moved, sem.at[1]),
-    ]
-    for copy in copies:
-        copy.start()
-    for copy in copies:
-        copy.wait()
+def hand_over(heated_in, moved_in, heated, moved, heated_here, moved_here, in_sem, out_sem):
+    ways = ((heated_in, heated_here, heated), (moved_in, moved_here, moved))
+    loads = [pltpu.make_async_copy(src, here, in_sem.at[k]) for k, (src, here, _) in enumerate(ways)]
+    stores = [pltpu.make_async_copy(here, dst, out_sem.at[k]) for k, (_, here, dst) in enumerate(ways)]
+    for load in loads:
+        load.start()
+    for load, store in zip(loads, stores):
+        load.wait()
+        store.start()
+    for store in stores:
+        store.wait()
 
 
 def body(sizes, *args):
@@ -956,7 +957,12 @@
         out_shape=shapes,
         in_specs=[anywhere] * 2,
         out_specs=(anywhere, anywhere),
-        scratch_shapes=[pltpu.SemaphoreType.DMA((2,))],
+        scratch_shapes=[
+            pltpu.VMEM(tile, f32),
+            pltpu.VMEM((3,) + tile, f32),
+            pltpu.SemaphoreType.DMA((2,)),
+            pltpu.SemaphoreType.DMA((2,)),
+        ],
         compiler_params=pltpu.CompilerParams(vmem_limit_bytes=60 * 1024 * 1024),
         name="hand_over",
     )(*results)

time: 55.4 us -> 45.6 us (0.82)
  Pallas kernels: 54.6 us -> 44.8 us
    pallas_call x1, Pallas kernels: 9.06 us -> 1.68 us  [body(): pl.pallas_call(hand_over, out_shape=shapes, in_specs=[anywhere] * 2, out_...]
    pallas_call x1, Pallas kernels: 45.6 us -> 43.1 us  [body(): pl.pallas_call(functools.partial(kernel, sizes), out_shape=shapes, in_spe...]
where the time goes in v4:
time: 45.6 us; the launch traced here: 45.4 us
  Pallas kernels  44.8 us (98%)
  between operations  0.64 us (1%)
    pallas_call x1, Pallas kernels, body(): pl.pallas_call(functools.partial(kernel, sizes), out_shape=shapes, in_spe...  43.1 us
    pallas_call x1, Pallas kernels, body(): pl.pallas_call(hand_over, out_shape=shapes, in_specs=[anywhere] * 2, out_...  1.68 us

profile of v4, /device:TPU:1, one launch (start us, length us, event | category | flops | bytes accessed | tf_op | source)
XLA Modules:
  0.0 45.4 jit_solution(18097112623472430143)
XLA Ops:
  0.6 43.1 %sections_and_kick.1 = (f32[16,8,128]{2,1,0:T(8,128)}, f32[3,16,8,128]{3,2,1,0:T(8,128)}) custom-call(s32[8,128]{1,0:T(8,128)} %pop_in.1, f32[3,16,8,128]{3,2,1,0:T(8,128)} %loc_in.1, f32[2,16,8,128]{3,2,1,0:T(8,128)} %tilt_in.1, f32[16,8,128]{2,1,0:T(8,128)} %mass_in.1, f32[16,8,128]{2,1,0:T(8,128)} %kappa_in.1, f32[16,8,128]{2,1,0:T(8,128)} %cap_in.1, ...), custom_call_target="tpu_custom_call" | custom-call | tf_op jit(solution)/shard_map/sections_and_kick/pallas_call | solution.py:943
  43.8 1.7 %hand_over.1 = (f32[16,8,128]{2,1,0:T(8,128)}, f32[3,16,8,128]{3,2,1,0:T(8,128)}) custom-call(f32[16,8,128]{2,1,0:T(8,128)} %get-tuple-element.4.heated_in, f32[3,16,8,128]{3,2,1,0:T(8,128)} %get-tuple-element.5.moved_in), custom_call_target="tpu_custom_call" | custom-call | tf_op jit(solution)/shard_map/hand_over/pallas_call | solution.py:955

commit v5 on v4

--- a/solution.py
+++ b/solution.py
@@ -606,19 +606,19 @@
         clear(p)
 
     def section_dirs(off, n, carry):
-        d = lax.div(n, 4)
-        p0 = lax.rem(n, 4) * 4
-        mine = [field[at(p0 + a), :] for a in range(4)]
-        ti = [zero] * 4
+        d = lax.div(n, 2)
+        p0 = lax.rem(n, 2) * 8
+        mine = [field[at(p0 + a), :] for a in range(8)]
+        ti = [zero] * 8
         for q in range(SLOTS):
             other = sfar[lax.rem(d, 3), partner(q, off), :]
             tj = None
-            for a in range(4):
+            for a in range(8):
                 t = store[CO, d * 256 + (p0 + a) * 16 + q] * (other - mine[a])
                 ti[a] = ti[a] + t
                 tj = t if tj is None else tj + t
             accj[d, 0, slot_sum(q), :] -= tj
-        for a in range(4):
+        for a in range(8):
             acc[0, at(p0 + a), :] += ti[a]
         return carry
 
@@ -644,16 +644,16 @@
         return lambda a, index: (store[CO, index] * (other - mine[a]),)
 
     def drag_dirs(off, n, carry):
-        d = lax.div(n, 8)
-        p0 = lax.rem(n, 8) * 2
-        g = [gfac[at(p0 + a), :] for a in range(2)]
-        v = [[own[VX + c, at(p0 + a), :] for c in range(3)] for a in range(2)]
-        total = [[zero] * 3 for _ in range(2)]
+        d = lax.div(n, 4)
+        p0 = lax.rem(n, 4) * 4
+        g = [gfac[at(p0 + a), :] for a in range(4)]
+        v = [[own[VX + c, at(p0 + a), :] for c in range(3)] for a in range(4)]
+        total = [[zero] * 3 for _ in range(4)]
         for q in range(SLOTS):
             gj = gfar[lax.rem(d, 3), partner(q, off), :]
             vj = [far[lax.rem(d, 3), VX + c, partner(q, off), :] for c in range(3)]
             back = [None] * 3
-            for a in range(2):
+            for a in range(4):
                 w = store[KE, d * 256 + (p0 + a) * 16 + q] * (g[a] * gj)
                 for c in range(3):
                     e = w * (vj[c] - v[a][c])
@@ -661,7 +661,7 @@
                     back[c] = e if back[c] is None else back[c] + e
             for c in range(3):
                 kaccj[d, c, slot_sum(q), :] -= back[c]
-        for a in range(2):
+        for a in range(4):
             for c in range(3):
                 kacc[c, at(p0 + a), :] += total[a][c]
         return carry
@@ -707,14 +707,14 @@
         )
 
     def push_dirs(off, n, carry):
-        d = lax.div(n, 8)
-        p0 = lax.rem(n, 8) * 2
-        pi = [field[at(p0 + a), :] for a in range(2)]
-        total = [[zero] * 3 for _ in range(2)]
+        d = lax.div(n, 4)
+        p0 = lax.rem(n, 4) * 4
+        pi = [field[at(p0 + a), :] for a in range(4)]
+        total = [[zero] * 3 for _ in range(4)]
         for q in range(SLOTS):
             pj = sfar[lax.rem(d, 3), partner(q, off), :]
             back = [None] * 3
-            for a in range(2):
+            for a in range(4):
                 both = pi[a] + pj
                 for c in range(3):
                     e = both * store[WX + c, d * 256 + (p0 + a) * 16 + q]
@@ -722,7 +722,7 @@
                     back[c] = e if back[c] is None else back[c] + e
             for c in range(3):
                 kaccj[d, c, slot_sum(q), :] -= back[c]
-        for a in range(2):
+        for a in range(4):
             for c in range(3):
                 kacc[c, at(p0 + a), :] += total[a][c]
         return carry
@@ -782,7 +782,7 @@
             copy.start()
 
         if e < 3:
-            over(section_dirs, 0, 16, 4)
+            over(section_dirs, 0, 8, 2)
             for p in range(SLOTS):
                 section_self(p)
 
@@ -793,10 +793,10 @@
             drag_rim()
 
         if e < 3:
-            over(drag_dirs, (0, 8, 20)[e], (8, 20, 32)[e], 8)
+            over(drag_dirs, (0, 4, 10)[e], (4, 10, 16)[e], 4)
 
         if e == 3:
-            over(push_dirs, 0, 32, 8)
+            over(push_dirs, 0, 16, 4)
             for p in range(SLOTS):
                 push_self(p)
 

time: 45.6 us -> 45.5 us (level)
  no operation moved by 1% of the time
where the time goes in v5:
time: 45.5 us; the launch traced here: 45.4 us
  Pallas kernels  44.8 us (98%)
  between operations  0.64 us (1%)
    pallas_call x1, Pallas kernels, body(): pl.pallas_call(functools.partial(kernel, sizes), out_shape=shapes, in_spe...  43.1 us
    pallas_call x1, Pallas kernels, body(): pl.pallas_call(hand_over, out_shape=shapes, in_specs=[anywhere] * 2, out_...  1.68 us

profile of v5, /device:TPU:1, one launch (start us, length us, event | category | flops | bytes accessed | tf_op | source)
XLA Modules:
  0.0 45.4 jit_solution(9300161962959476488)
XLA Ops:
  0.6 43.1 %sections_and_kick.1 = (f32[16,8,128]{2,1,0:T(8,128)}, f32[3,16,8,128]{3,2,1,0:T(8,128)}) custom-call(s32[8,128]{1,0:T(8,128)} %pop_in.1, f32[3,16,8,128]{3,2,1,0:T(8,128)} %loc_in.1, f32[2,16,8,128]{3,2,1,0:T(8,128)} %tilt_in.1, f32[16,8,128]{2,1,0:T(8,128)} %mass_in.1, f32[16,8,128]{2,1,0:T(8,128)} %kappa_in.1, f32[16,8,128]{2,1,0:T(8,128)} %cap_in.1, ...), custom_call_target="tpu_custom_call" | custom-call | tf_op jit(solution)/shard_map/sections_and_kick/pallas_call | solution.py:943
  43.7 1.7 %hand_over.1 = (f32[16,8,128]{2,1,0:T(8,128)}, f32[3,16,8,128]{3,2,1,0:T(8,128)}) custom-call(f32[16,8,128]{2,1,0:T(8,128)} %get-tuple-element.4.heated_in, f32[3,16,8,128]{3,2,1,0:T(8,128)} %get-tuple-element.5.moved_in), custom_call_target="tpu_custom_call" | custom-call | tf_op jit(solution)/shard_map/hand_over/pallas_call | solution.py:955
